TPU v7x, 128 devices: a whole 4x4x4 slice. The times are simulated.
128 devices in a mesh: ctx: 32 (over y, z_hi, x), tp: 4 (over z_lo, core).
Axes of the slice: x: 4, y: 4, z: 4 (z_hi: 2, z_lo: 2; z = z_hi * 2 + z_lo), core: 2. Of those that a mesh axis runs over, the one named last changes fastest.
Arguments:
- query_rot: bfloat16 [16384, 3072], P('ctx', 'tp'), may hold values from -12 to 12
- key_rot: bfloat16 [16384, 3072], P('ctx', 'tp'), may hold values from -12 to 12
- value: bfloat16 [16384, 3072], P('ctx', 'tp'), may hold values from -6 to 6
- grad_out: bfloat16 [16384, 3072], P('ctx', 'tp'), may hold values from -6 to 6
- text_key: bfloat16 [256, 3072], P('ctx', 'tp'), may hold values from -6 to 6
- text_value: bfloat16 [256, 3072], P('ctx', 'tp'), may hold values from -6 to 6
- positions: int32 [3, 16384], P(None, 'ctx'), may hold values from 0 to 63, as said below
- tile_mask: int32 [128, 128], replicated, may hold values from 0 to 1, as said below
Outputs:
- grad_query: bfloat16 [16384, 3072], P('ctx', 'tp')
- grad_key: bfloat16 [16384, 3072], P('ctx', 'tp')
- grad_value: bfloat16 [16384, 3072], P('ctx', 'tp')
- grad_text_key: bfloat16 [256, 3072], P('ctx', 'tp')
- grad_text_value: bfloat16 [256, 3072], P('ctx', 'tp')
Inputs may be any that keep to these rules, and one draw needn't show every extreme that they name: tile_mask[a, b] is 1 when tiles a and b lie in the same frame (2 tiles a frame, in token order) and 0 when their frames are more than 2 apart. positions[0, n] is n // 256; positions[1, n] and positions[2, n] are the row and column of token n in its frame of rows of 16 tokens, each plus an offset of 0 to 31 common to all tokens.
All inputs are finite; a program needn't handle non-finite values.
Results may differ from a plain program's by a relative error of at most 0.02.
Values may be sent and summed in bfloat16 or wider, within the bound.
No kernel may reach another device: no remote copies, remote signals or barrier semaphores. Data moves between devices by JAX's collectives and lax.ppermute only.
A program may use at most 128 MiB of HBM per device.

v0:
```python
import jax
import jax.numpy as jnp
from jax import lax
from jax.sharding import PartitionSpec as P

D_HEAD = 128
TILE = 128


ROPE_THETA = 256.0
TIME_STRETCH = 0.25


def shifted(block, axis, distance):
    devices = range(lax.axis_size(axis))
    route = [(i - distance, i) for i in devices if i - distance in devices]
    return lax.ppermute(block, axis, route)


def rope_tables(positions, head_dim):
    time_dims = head_dim // 8
    plane_dims = (head_dim - time_dims) // 2
    layout = ((time_dims, TIME_STRETCH), (plane_dims, 1.0), (plane_dims, 1.0))
    angle_parts = []
    for axis_id in range(3):
        seg_width, stretch = layout[axis_id]
        pair_ids = jnp.arange(seg_width // 2, dtype=jnp.float32)
        frequency = ROPE_THETA ** (-2.0 * pair_ids / seg_width)
        scaled_pos = positions[axis_id].astype(jnp.float32) * stretch
        angle_parts.append(scaled_pos[:, None] * frequency[None, :])
    angles = jnp.concatenate(angle_parts, axis=1)
    return (jnp.cos(angles), jnp.sin(angles))


def unrotate(grad_rot, cosine, sine):
    tok_rows = grad_rot.shape[0]
    pairs = grad_rot.reshape(tok_rows, -1, cosine.shape[1], 2)
    even_part = pairs[..., 0]
    odd_part = pairs[..., 1]
    cos_rows = cosine[:, None, :]
    sin_rows = sine[:, None, :]
    turned = jnp.stack(
        [cos_rows * even_part + sin_rows * odd_part, cos_rows * odd_part - sin_rows * even_part],
        axis=-1,
    )
    return turned.reshape(grad_rot.shape)


def scores_of(query_head, key_head):
    return jnp.einsum(
        "qd,kd->qk", query_head, key_head, preferred_element_type=jnp.float32
    ) * D_HEAD ** (-0.5)


def piece_grads(query_head, grad_head, weights, row_delta, key_head, value_head):
    score_scale = D_HEAD ** (-0.5)
    dprobs = jnp.einsum("qd,kd->qk", grad_head, value_head, preferred_element_type=jnp.float32)
    dscores = (weights.astype(jnp.float32) * (dprobs - row_delta[:, None])).astype(jnp.bfloat16)
    results = []
    results.append(jnp.dot(dscores, key_head, preferred_element_type=jnp.float32) * score_scale)
    results.append(
        jnp.einsum("qk,qd->kd", dscores, query_head, preferred_element_type=jnp.float32)
        * score_scale
    )
    results.append(jnp.einsum("qk,qd->kd", weights, grad_head, preferred_element_type=jnp.float32))
    return tuple(results)


def shards(query_rot, key_rot, value, grad_out, text_key, text_value, positions, tile_mask):
    tok_rows = query_rot.shape[0]
    head_count = query_rot.shape[1] // D_HEAD
    tile_rows = tok_rows // TILE
    ctx_index = lax.axis_index("ctx")
    text_keys, text_values = (
        lax.all_gather(text_key, "ctx", axis=0, tiled=True),
        lax.all_gather(text_value, "ctx", axis=0, tiled=True),
    )
    left_keys, left_values = shifted((key_rot, value), "ctx", 1)
    right_keys, right_values = shifted((key_rot, value), "ctx", -1)
    padded_mask = jnp.pad(tile_mask, ((tile_rows, tile_rows), (tile_rows, tile_rows)))

    def window(col_shift):
        mask_block = lax.dynamic_slice(
            padded_mask,
            ((ctx_index + 1) * tile_rows, (ctx_index + col_shift + 1) * tile_rows),
            (tile_rows, tile_rows),
        )
        return jnp.repeat(jnp.repeat(mask_block, TILE, axis=0), TILE, axis=1) > 0

    allow_left = window(-1)
    allow_own = window(0)
    allow_right = window(1)
    query_parts, own_key_parts, own_value_parts = ([], [], [])
    left_key_parts, left_value_parts, right_key_parts, right_value_parts = ([], [], [], [])
    text_key_parts, text_value_parts, total_parts, delta_parts = ([], [], [], [])
    for head_id in range(head_count):
        head_cols = slice(head_id * D_HEAD, (head_id + 1) * D_HEAD)
        query_head = query_rot[:, head_cols]
        grad_head = grad_out[:, head_cols]
        text_key_head = text_keys[:, head_cols]
        text_value_head = text_values[:, head_cols]
        sides = (
            (left_keys[:, head_cols], left_values[:, head_cols], allow_left),
            (key_rot[:, head_cols], value[:, head_cols], allow_own),
            (right_keys[:, head_cols], right_values[:, head_cols], allow_right),
        )
        masked = []
        for key_head, value_head, allowed in sides:
            masked.append(jnp.where(allowed, scores_of(query_head, key_head), -jnp.inf))
        text_scores = scores_of(query_head, text_key_head)
        row_max = jnp.max(text_scores, axis=1)
        for piece_scores in masked:
            row_max = jnp.maximum(row_max, jnp.max(piece_scores, axis=1))
        row_total = jnp.sum(jnp.exp(text_scores - row_max[:, None]), axis=1)
        for piece_scores in masked:
            row_total = row_total + jnp.sum(jnp.exp(piece_scores - row_max[:, None]), axis=1)
        log_total = row_max + jnp.log(row_total)
        weight_list = [
            jnp.exp(piece_scores - log_total[:, None]).astype(jnp.bfloat16)
            for piece_scores in masked
        ]
        text_weights = jnp.exp(text_scores - log_total[:, None]).astype(jnp.bfloat16)
        attended = jnp.dot(text_weights, text_value_head, preferred_element_type=jnp.float32)
        for slot in range(3):
            attended = attended + jnp.dot(
                weight_list[slot], sides[slot][1], preferred_element_type=jnp.float32
            )
        row_delta = jnp.sum(grad_head.astype(jnp.float32) * attended, axis=1)
        total_parts.append(log_total)
        delta_parts.append(row_delta)
        text_terms = piece_grads(
            query_head, grad_head, text_weights, row_delta, text_key_head, text_value_head
        )
        query_grad = text_terms[0]
        text_key_parts.append(text_terms[1])
        text_value_parts.append(text_terms[2])
        for slot in range(3):
            key_head, value_head, allowed = sides[slot]
            terms = piece_grads(
                query_head, grad_head, weight_list[slot], row_delta, key_head, value_head
            )
            query_grad = query_grad + terms[0]
            if slot == 0:
                left_key_parts.append(terms[1])
                left_value_parts.append(terms[2])
            if slot == 1:
                own_key_parts.append(terms[1])
                own_value_parts.append(terms[2])
            if slot == 2:
                right_key_parts.append(terms[1])
                right_value_parts.append(terms[2])
        query_parts.append(query_grad)
    query_grad_all = jnp.concatenate(query_parts, axis=1)
    key_grad_all = jnp.concatenate(own_key_parts, axis=1)
    value_grad_all = jnp.concatenate(own_value_parts, axis=1)
    right_back = (
        shifted(jnp.concatenate(left_key_parts, axis=1).astype(jnp.bfloat16), "ctx", -1).astype(
            jnp.float32
        ),
        shifted(jnp.concatenate(left_value_parts, axis=1).astype(jnp.bfloat16), "ctx", -1).astype(
            jnp.float32
        ),
    )
    left_back = (
        shifted(jnp.concatenate(right_key_parts, axis=1).astype(jnp.bfloat16), "ctx", 1).astype(
            jnp.float32
        ),
        shifted(jnp.concatenate(right_value_parts, axis=1).astype(jnp.bfloat16), "ctx", 1).astype(
            jnp.float32
        ),
    )
    key_grad_all = key_grad_all + right_back[0] + left_back[0]
    value_grad_all = value_grad_all + right_back[1] + left_back[1]
    text_key_grad, text_value_grad = (
        lax.psum_scatter(
            jnp.concatenate(text_key_parts, axis=1).astype(jnp.bfloat16),
            "ctx",
            scatter_dimension=0,
            tiled=True,
        ).astype(jnp.float32),
        lax.psum_scatter(
            jnp.concatenate(text_value_parts, axis=1).astype(jnp.bfloat16),
            "ctx",
            scatter_dimension=0,
            tiled=True,
        ).astype(jnp.float32),
    )
    cosine, sine = rope_tables(positions, D_HEAD)
    grad_query = unrotate(query_grad_all, cosine, sine).astype(jnp.bfloat16)
    grad_key = unrotate(key_grad_all, cosine, sine).astype(jnp.bfloat16)
    return (
        grad_query,
        grad_key,
        value_grad_all.astype(jnp.bfloat16),
        text_key_grad.astype(jnp.bfloat16),
        text_value_grad.astype(jnp.bfloat16),
    )


def solution(mesh):
    placed = (
        P("ctx", "tp"),
        P("ctx", "tp"),
        P("ctx", "tp"),
        P("ctx", "tp"),
        P("ctx", "tp"),
        P("ctx", "tp"),
        P(None, "ctx"),
        P(),
    )
    return jax.shard_map(
        shards,
        mesh=mesh,
        in_specs=placed,
        out_specs=(P("ctx", "tp"), P("ctx", "tp"), P("ctx", "tp"), P("ctx", "tp"), P("ctx", "tp")),
        check_vma=False,
    )
```

profile of v0, /device:TPU:15, one launch (start us, length us, event | category | flops | bytes accessed | tf_op | source)
XLA Modules:
  0.0 771.6 jit_solution(6786113106563927850)
XLA Ops:
  7.3 2.6 collective-permute-start.1
  9.9 6.4 collective-permute-start
  16.3 1.9 collective-permute-start.2
  18.2 3.4 collective-permute-start.3
  21.6 88.8 %all_gather.6 = bf16[256,768]{1,0:T(8,128)(2,1)S(1)} all-gather(bf16[8,768]{1,0:T(8,128)(2,1)} %param.12), channel_id=1, replica_groups=mesh['ctx'=32,'tp'=4] {'ctx'}, dimensions={0}, use_global_device_ids=true | all-gather | bytes 405504 | tf_op jit(solution)/shard_map/all_gather | solution.py:75
  110.5 1.9 fusion.352
  112.4 1.7 fusion.348
  114.1 1.6 fusion.344
  117.7 70.8 %all_gather.7 = bf16[256,768]{1,0:T(8,128)(2,1)} all-gather(bf16[8,768]{1,0:T(8,128)(2,1)S(1)} %copy-done.75), channel_id=1, replica_groups=mesh['ctx'=32,'tp'=4] {'ctx'}, dimensions={0}, use_global_device_ids=true | all-gather | bytes 405504 | tf_op jit(solution)/shard_map/all_gather | solution.py:76
  190.7 1.9 fusion.351
  192.6 1.9 fusion.347
  194.5 1.8 fusion.343
  196.3 1.9 fusion.355
  198.2 1.8 fusion.359
  200.0 2.2 fusion.363
  202.2 1.7 copy.156
  203.9 1.7 copy.155
  205.5 1.7 copy.157
  207.2 1.7 copy.158
  208.9 1.7 copy.159
  210.5 1.7 copy.160
  212.9 1.3 fusion.346
  216.7 1.5 fusion.345
  220.7 1.5 fusion.350
  224.2 1.3 fusion.354
  230.5 1.3 fusion.362
  235.8 1.4 convolution_add_fusion.5
  274.8 1.9 copy.153
  278.0 1.9 fusion.130
  286.9 3.7 collective-permute-start.6
  297.2 5.5 collective-permute-start.7
  303.3 1.2 fusion.35
  316.0 1.3 fusion.20
  318.3 2.5 collective-permute-start.4
  324.5 1.4 fusion.33
  326.2 1.2 convolution_add_fusion.2
  338.4 1.4 fusion.56
  348.4 2.2 reshape.347
  350.6 6.8 collective-permute-start.5
  357.4 2.2 fusion.50
  359.6 2.1 fusion.49
  362.8 1.8 add_convert_fusion
  366.6 3.3 convert_add_fusion
  369.9 2.3 reshape.348
  372.2 4.3 add_convert_fusion.1
  376.5 3.6 pad_maximum_fusion
  383.0 157.5 %reduce-scatter.9.cloned.1.call-done = bf16[8,768]{1,0:T(8,128)(2,1)} async-done(((bf16[256,768]{1,0:T(8,128)(2,1)}), bf16[8,768]{1,0:T(8,128)(2,1)}) %reduce-scatter.9.cloned.1.call-update) | async-done | bytes 12304
  540.5 223.8 %reduce-scatter.7.cloned.1.call-done = bf16[8,768]{1,0:T(8,128)(2,1)} async-done(((bf16[256,768]{1,0:T(8,128)(2,1)}), bf16[8,768]{1,0:T(8,128)(2,1)}) %reduce-scatter.7.cloned.1.call-update) | async-done | bytes 12304
  (365 shorter events, 114.3 us)
Async XLA Ops:
  7.2 107.0 %copy-start.1 = (bf16[512,768]{1,0:T(8,128)(2,1)S(1)}, bf16[512,768]{1,0:T(8,128)(2,1)}, u32[]{:S(2)}) copy-start(bf16[512,768]{1,0:T(8,128)(2,1)} %param.8) | copy-start | bytes 2359300
  7.2 108.6 %copy-start.85 = (s32[3,512]{1,0:T(4,128)S(1)}, s32[3,512]{1,0:T(4,128)}, u32[]{:S(2)}) copy-start(s32[3,512]{1,0:T(4,128)} %param.14) | copy-start | bytes 18436
  7.2 108.6 %copy-start.69 = (s32[128,128]{1,0:T(8,128)S(1)}, s32[128,128]{1,0:T(8,128)}, u32[]{:S(2)}) copy-start(s32[128,128]{1,0:T(8,128)} %param.15) | copy-start | bytes 196612
  7.2 110.5 %copy-start.75 = (bf16[8,768]{1,0:T(8,128)(2,1)S(1)}, bf16[8,768]{1,0:T(8,128)(2,1)}, u32[]{:S(2)}) copy-start(bf16[8,768]{1,0:T(8,128)(2,1)} %param.13) | copy-start | bytes 36868
  7.2 181.3 %copy-start = (bf16[512,768]{1,0:T(8,128)(2,1)S(1)}, bf16[512,768]{1,0:T(8,128)(2,1)}, u32[]{:S(2)}) copy-start(bf16[512,768]{1,0:T(8,128)(2,1)} %param.11) | copy-start | bytes 2359300
  7.2 533.3 %reduce-scatter.9.cloned.1.call-start = ((), (), s32[]{:S(2)}) async-start(), calls=%async_computation.3 | async-start | bytes 405504
  7.3 205.7 %collective-permute-start.1 = (bf16[512,768]{1,0:T(8,128)(2,1)}, bf16[512,768]{1,0:T(8,128)(2,1)}, u32[]{:S(2)}, u32[]{:S(2)}) collective-permute-start(bf16[512,768]{1,0:T(8,128)(2,1)} %param.9), channel_id=1, source_target_pairs={{4,0},{8,4},{12,8},{16,12},{20,16},{24,20},{28,24},{32,28},{36,32}... | collective-permute-start | bytes 2359304 | tf_op jit(solution)/shard_map/ppermute | solution.py:17
  9.9 204.4 %collective-permute-start = (bf16[512,768]{1,0:T(8,128)(2,1)}, bf16[512,768]{1,0:T(8,128)(2,1)}, u32[]{:S(2)}, u32[]{:S(2)}) collective-permute-start(bf16[512,768]{1,0:T(8,128)(2,1)} %param.9), channel_id=1, source_target_pairs={{0,4},{4,8},{8,12},{12,16},{16,20},{20,24},{24,28},{28,32},{32,36}... | collective-permute-start | bytes 2359304 | tf_op jit(solution)/shard_map/ppermute | solution.py:17
  16.3 219.5 %collective-permute-start.2 = (bf16[512,768]{1,0:T(8,128)(2,1)}, bf16[512,768]{1,0:T(8,128)(2,1)}, u32[]{:S(2)}, u32[]{:S(2)}) collective-permute-start(bf16[512,768]{1,0:T(8,128)(2,1)} %param.10), channel_id=1, source_target_pairs={{0,4},{4,8},{8,12},{12,16},{16,20},{20,24},{24,28},{28,32},{32,36}... | collective-permute-start | bytes 2359304 | tf_op jit(solution)/shard_map/ppermute | solution.py:17
  18.2 221.2 %collective-permute-start.3 = (bf16[512,768]{1,0:T(8,128)(2,1)}, bf16[512,768]{1,0:T(8,128)(2,1)}, u32[]{:S(2)}, u32[]{:S(2)}) collective-permute-start(bf16[512,768]{1,0:T(8,128)(2,1)} %param.10), channel_id=1, source_target_pairs={{4,0},{8,4},{12,8},{16,12},{20,16},{24,20},{28,24},{32,28},{36,32}... | collective-permute-start | bytes 2359304 | tf_op jit(solution)/shard_map/ppermute | solution.py:17
  114.1 76.6 %copy-start.50 = (bf16[512,768]{1,0:T(8,128)(2,1)S(1)}, bf16[512,768]{1,0:T(8,128)(2,1)}, u32[]{:S(2)}) copy-start(bf16[512,768]{1,0:T(8,128)(2,1)} %param.9) | copy-start | bytes 2359300
  198.2 4.1 copy-start.83
  198.2 4.1 copy-start.84
  216.7 40.4 %copy-start.9 = (bf16[512,512]{0,1:T(8,128)(2,1)}, bf16[512,512]{0,1:T(8,128)(2,1)S(1)}, u32[]{:S(2)}) copy-start(bf16[512,512]{0,1:T(8,128)(2,1)S(1)} %get-tuple-element.71) | copy-start | bytes 1572868
  216.7 44.0 %copy-start.11 = (bf16[512,512]{0,1:T(8,128)(2,1)}, bf16[512,512]{0,1:T(8,128)(2,1)S(1)}, u32[]{:S(2)}) copy-start(bf16[512,512]{0,1:T(8,128)(2,1)S(1)} %get-tuple-element.70) | copy-start | bytes 1572868
  220.7 43.0 %copy-start.13 = (bf16[512,512]{0,1:T(8,128)(2,1)}, bf16[512,512]{0,1:T(8,128)(2,1)S(1)}, u32[]{:S(2)}) copy-start(bf16[512,512]{0,1:T(8,128)(2,1)S(1)} %get-tuple-element.74) | copy-start | bytes 1572868
  220.7 45.5 %copy-start.7 = (bf16[512,512]{0,1:T(8,128)(2,1)}, bf16[512,512]{0,1:T(8,128)(2,1)S(1)}, u32[]{:S(2)}) copy-start(bf16[512,512]{0,1:T(8,128)(2,1)S(1)} %get-tuple-element.72) | copy-start | bytes 1572868
  235.1 17.7 %copy-start.25 = (bf16[512,512]{0,1:T(8,128)(2,1)}, bf16[512,512]{0,1:T(8,128)(2,1)S(1)}, u32[]{:S(2)}) copy-start(bf16[512,512]{0,1:T(8,128)(2,1)S(1)} %get-tuple-element.68) | copy-start | bytes 1572868
  235.1 19.1 %copy-start.17 = (bf16[512,512]{0,1:T(8,128)(2,1)}, bf16[512,512]{0,1:T(8,128)(2,1)S(1)}, u32[]{:S(2)}) copy-start(bf16[512,512]{0,1:T(8,128)(2,1)S(1)} %get-tuple-element.66) | copy-start | bytes 1572868
  235.1 20.6 %copy-start.33 = (bf16[512,512]{0,1:T(8,128)(2,1)}, bf16[512,512]{0,1:T(8,128)(2,1)S(1)}, u32[]{:S(2)}) copy-start(bf16[512,512]{0,1:T(8,128)(2,1)S(1)} %get-tuple-element.67) | copy-start | bytes 1572868
  235.8 6.4 copy-start.31
  238.9 9.6 %copy-start.27 = (bf16[512,512]{0,1:T(8,128)(2,1)}, bf16[512,512]{0,1:T(8,128)(2,1)S(1)}, u32[]{:S(2)}) copy-start(bf16[512,512]{0,1:T(8,128)(2,1)S(1)} %get-tuple-element.65) | copy-start | bytes 1572868
  238.9 11.0 %copy-start.19 = (bf16[512,512]{0,1:T(8,128)(2,1)}, bf16[512,512]{0,1:T(8,128)(2,1)S(1)}, u32[]{:S(2)}) copy-start(bf16[512,512]{0,1:T(8,128)(2,1)S(1)} %get-tuple-element.63) | copy-start | bytes 1572868
  239.0 12.4 %copy-start.35 = (bf16[512,512]{0,1:T(8,128)(2,1)}, bf16[512,512]{0,1:T(8,128)(2,1)S(1)}, u32[]{:S(2)}) copy-start(bf16[512,512]{0,1:T(8,128)(2,1)S(1)} %get-tuple-element.64) | copy-start | bytes 1572868
  239.5 4.1 copy-start.29
  239.5 5.5 copy-start.21
  239.5 7.7 copy-start.37
  259.7 4.0 copy-start.70
  276.7 5.3 copy-start.10
  276.7 487.6 %reduce-scatter.7.cloned.1.call-start = ((), (), s32[]{:S(2)}) async-start(), calls=%async_computation.2 | async-start | bytes 405504
  278.0 5.0 copy-start.26
  283.0 7.6 copy-start.12
  283.0 7.6 copy-start.55
  284.0 7.0 copy-start.34
  284.9 6.3 copy-start.36
  285.9 5.7 copy-start.38
  286.9 75.8 %collective-permute-start.6 = (bf16[512,768]{0,1:T(8,128)(2,1)}, bf16[512,768]{0,1:T(8,128)(2,1)}, u32[]{:S(2)}, u32[]{:S(2)}) collective-permute-start(bf16[512,768]{0,1:T(8,128)(2,1)} %fusion.102), channel_id=1, source_target_pairs={{4,0},{8,4},{12,8},{16,12},{20,16},{24,20},{28,24},{32,28},{36,32}... | collective-permute-start | bytes 2359304 | tf_op jit(solution)/shard_map/ppermute | solution.py:17
  293.3 9.4 %copy-start.52 = (bf16[512,256]{0,1:T(8,128)(2,1)S(1)}, bf16[512,256]{0,1:T(8,128)(2,1)}, u32[]{:S(2)}) copy-start(bf16[512,256]{0,1:T(8,128)(2,1)} %fusion.42) | copy-start | bytes 786436
  294.3 8.7 %copy-start.53 = (bf16[512,256]{0,1:T(8,128)(2,1)S(1)}, bf16[512,256]{0,1:T(8,128)(2,1)}, u32[]{:S(2)}) copy-start(bf16[512,256]{0,1:T(8,128)(2,1)} %fusion.43) | copy-start | bytes 786436
  294.3 9.0 %copy-start.14 = (bf16[512,512]{0,1:T(8,128)(2,1)S(1)}, bf16[512,512]{0,1:T(8,128)(2,1)}, u32[]{:S(2)}) copy-start(bf16[512,512]{0,1:T(8,128)(2,1)} %copy-done.13) | copy-start | bytes 1572868
  294.3 9.0 %copy-start.73 = (f32[512]{0:T(512)S(1)}, f32[512]{0:T(512)}, u32[]{:S(2)}) copy-start(f32[512]{0:T(512)} %copy-done.72) | copy-start | bytes 6148
  297.2 8.3 %copy-start.45 = (bf16[512,512]{0,1:T(8,128)(2,1)S(1)}, bf16[512,512]{0,1:T(8,128)(2,1)}, u32[]{:S(2)}) copy-start(bf16[512,512]{0,1:T(8,128)(2,1)} %fusion.34) | copy-start | bytes 1572868
  297.2 65.5 %collective-permute-start.7 = (bf16[512,768]{0,1:T(8,128)(2,1)}, bf16[512,768]{0,1:T(8,128)(2,1)}, u32[]{:S(2)}, u32[]{:S(2)}) collective-permute-start(bf16[512,768]{0,1:T(8,128)(2,1)} %fusion.96), channel_id=1, source_target_pairs={{0,4},{4,8},{8,12},{12,16},{16,20},{20,24},{24,28},{28,32},{32,36}... | collective-permute-start | bytes 2359304 | tf_op jit(solution)/shard_map/ppermute | solution.py:17
  316.0 5.9 copy-start.44
  318.3 47.4 %collective-permute-start.4 = (bf16[512,768]{0,1:T(8,128)(2,1)}, bf16[512,768]{0,1:T(8,128)(2,1)}, u32[]{:S(2)}, u32[]{:S(2)}) collective-permute-start(bf16[512,768]{0,1:T(8,128)(2,1)} %fusion.83), channel_id=1, source_target_pairs={{4,0},{8,4},{12,8},{16,12},{20,16},{24,20},{28,24},{32,28},{36,32}... | collective-permute-start | bytes 2359304 | tf_op jit(solution)/shard_map/ppermute | solution.py:17
  350.6 11.1 %copy-start.40 = (bf16[512,512]{0,1:T(8,128)(2,1)S(1)}, bf16[512,512]{0,1:T(8,128)(2,1)}, u32[]{:S(2)}) copy-start(bf16[512,512]{0,1:T(8,128)(2,1)} %fusion.19) | copy-start | bytes 1572868
  350.6 15.9 %collective-permute-start.5 = (bf16[512,768]{0,1:T(8,128)(2,1)}, bf16[512,768]{0,1:T(8,128)(2,1)}, u32[]{:S(2)}, u32[]{:S(2)}) collective-permute-start(bf16[512,768]{0,1:T(8,128)(2,1)} %copy-done.74), channel_id=1, source_target_pairs={{0,4},{4,8},{8,12},{12,16},{16,20},{20,24},{24,28},{28,32},{32,36}... | collective-permute-start | bytes 2359304 | tf_op jit(solution)/shard_map/ppermute | solution.py:17
  357.4 5.3 copy-start.57
  (48 other events, 126.9 us)
Sparse Core Ops, SparseCore 0:
  276.8 263.6 reduce-scatter.8
  546.6 217.6 reduce-scatter.6
where the time goes:
time: 787 us; the launch traced here: 772 us
  waiting for transfers between devices  382 us (49%)
  blocking collectives  160 us (20%)
  matrix products  133 us (17%)
  starting transfers between devices  32.9 us (4%)
  local copies, waits for them, and re-layouts  26.5 us (3%)
  other arithmetic  21.4 us (3%)
  between operations  16.4 us (2%)
    unnamed x4, waiting for transfers between devices  381 us
    all_gather x1, blocking collectives, shards(): lax.all_gather(text_key, 'ctx', axis=0, tiled=True)  88.8 us
    all_gather x1, blocking collectives, shards(): lax.all_gather(text_value, 'ctx', axis=0, tiled=True)  70.8 us
    dot_general x24, matrix products, scores_of(): jnp.einsum('qd,kd->qk', query_head, key_head, preferred_element_type=jnp....  32.9 us
    ppermute x8, starting transfers between devices, shifted(): return lax.ppermute(block, axis, route)  32.8 us
    dot_general x24, matrix products, piece_grads(): jnp.einsum('qd,kd->qk', grad_head, value_head, preferred_element_type=jnp...  24.8 us
    unnamed x190, local copies, waits for them, and re-layouts  21.1 us
    dot_general x24, matrix products, piece_grads(): jnp.einsum('qk,qd->kd', weights, grad_head, preferred_element_type=jnp.fl...  19.3 us
  transfers between devices with their start and end apart: 10, of which 3 were waited for; matrix products, arithmetic and copies ran while one was open for 18% of the time, Pallas kernels for 0%

commit v1 on v0

v1 whole, which is shorter than its diff:
```python
import functools
import math

import jax
import jax.numpy as jnp
from jax import lax
from jax.experimental import pallas as pl
from jax.experimental.pallas import tpu as pltpu
from jax.sharding import PartitionSpec as P

D_HEAD = 128
TILE = 128
FRAME = 256
ROPE_THETA = 256.0
TIME_STRETCH = 0.25
SCALE = D_HEAD ** (-0.5)
EXP2_SCALE = SCALE * math.log2(math.e)
BLOCKED = 1e30
GROUPS = 2
NT = (((1,), (1,)), ((), ()))
NN = (((1,), (0,)), ((), ()))
TN = (((0,), (0,)), ((), ()))


def shifted(block, axis, distance):
    devices = range(lax.axis_size(axis))
    route = [(i - distance, i) for i in devices if i - distance in devices]
    return lax.ppermute(block, axis, route)


def rope_tables(positions):
    time_dims = D_HEAD // 8
    plane_dims = (D_HEAD - time_dims) // 2
    layout = ((time_dims, TIME_STRETCH), (plane_dims, 1.0), (plane_dims, 1.0))
    angle_parts = []
    for axis_id in range(3):
        seg_width, stretch = layout[axis_id]
        pair_ids = (jnp.arange(seg_width, dtype=jnp.int32) // 2).astype(jnp.float32)
        frequency = ROPE_THETA ** (-2.0 * pair_ids / seg_width)
        scaled_pos = positions[axis_id].astype(jnp.float32) * stretch
        angle_parts.append(scaled_pos[:, None] * frequency[None, :])
    angles = jnp.concatenate(angle_parts, axis=1)
    odd = jnp.arange(D_HEAD, dtype=jnp.int32)[None, :] % 2 == 1
    sine = jnp.sin(angles)
    return jnp.cos(angles), jnp.where(odd, -sine, sine)


def unrotate(grad, cosine, sine):
    lane = lax.broadcasted_iota(jnp.int32, grad.shape, 1)
    partner = jnp.where(lane % 2 == 0, pltpu.roll(grad, D_HEAD - 1, 1), pltpu.roll(grad, 1, 1))
    return cosine * grad + sine * partner


def dot(lhs, rhs, dims):
    return lax.dot_general(lhs, rhs, dims, preferred_element_type=jnp.float32)


def fold_rows(block, combine):
    return combine(block.reshape(block.shape[0] // 8, 8, block.shape[1]), axis=0)


def attend_body(*refs, aliased):
    (bias_ref, cos_ref, sin_ref, q_ref, g_ref, ko_ref, vo_ref, kl_ref, vl_ref, kr_ref, vr_ref, tk_ref, tv_ref) = refs[:13]
    refs = refs[13 + (1 if aliased else 0):]
    dq_ref, dko_ref, dvo_ref, dl_ref, dr_ref, dt_ref, s_scr, dp_scr, e_scr = refs
    tok = q_ref.shape[0]
    f = FRAME
    chunks = (
        (kl_ref, vl_ref, 0, (0,), 0),
        (kl_ref, vl_ref, f, (0, 1), 2),
        (ko_ref, vo_ref, 0, (0, 1), 4),
        (ko_ref, vo_ref, f, (0, 1), 6),
        (kr_ref, vr_ref, 0, (0, 1), 8),
        (kr_ref, vr_ref, f, (1,), 10),
        (tk_ref, tv_ref, 0, (0, 1), None),
    )
    inv_rows, delta_rows, q_scaled, g_scaled = [], [], [], []
    for frame in range(2):
        cols = slice(frame * f, (frame + 1) * f)
        query = q_ref[cols, :]
        grad = g_ref[cols, :]
        top = None
        for c, (k_ref, _, row, frames, tile) in enumerate(chunks):
            if frame not in frames:
                continue
            scores = dot(k_ref[row:row + f, :], query, NT)
            s_scr[c * f:(c + 1) * f, cols] = scores
            for t in range(2):
                part = fold_rows(scores[t * TILE:(t + 1) * TILE], jnp.max)
                if tile is not None:
                    part = part - bias_ref[tile + t:tile + t + 1, cols]
                top = part if top is None else jnp.maximum(top, part)
        top = jnp.max(top, axis=0, keepdims=True) * EXP2_SCALE
        total = jnp.zeros((8, f), jnp.float32)
        delta = jnp.zeros((8, f), jnp.float32)
        for c, (_, v_ref, row, frames, tile) in enumerate(chunks):
            if frame not in frames:
                continue
            dprobs = dot(v_ref[row:row + f, :], grad, NT)
            dp_scr[c * f:(c + 1) * f, cols] = dprobs
            for t in range(2):
                rows = slice(c * f + t * TILE, c * f + (t + 1) * TILE)
                shift = top
                if tile is not None:
                    shift = shift + bias_ref[tile + t:tile + t + 1, cols]
                weights = jnp.exp2(s_scr[rows, cols] * EXP2_SCALE - shift)
                e_scr[rows, cols] = weights.astype(jnp.bfloat16)
                total = total + fold_rows(weights, jnp.sum)
                delta = delta + fold_rows(weights * dprobs[t * TILE:(t + 1) * TILE], jnp.sum)
        inv = 1.0 / jnp.sum(total, axis=0, keepdims=True)
        delta_rows.append(jnp.sum(delta, axis=0, keepdims=True) * inv)
        inv_rows.append(inv)
        inv_col = jnp.transpose(jnp.broadcast_to(inv, (D_HEAD, f)))
        q_scaled.append((query.astype(jnp.float32) * (inv_col * SCALE)).astype(jnp.bfloat16))
        g_scaled.append((grad.astype(jnp.float32) * inv_col).astype(jnp.bfloat16))
    q_both = jnp.concatenate(q_scaled, axis=0)
    g_both = jnp.concatenate(g_scaled, axis=0)
    delta_both = jnp.concatenate(delta_rows, axis=1)
    inv_both = jnp.concatenate(inv_rows, axis=1)
    dq_parts = [jnp.zeros((D_HEAD, f), jnp.float32) for _ in range(2)]
    outs = (
        (dl_ref, 0, tok), (dl_ref, f, tok + f),
        (dko_ref, 0, None), (dko_ref, f, None),
        (dr_ref, 0, tok), (dr_ref, f, tok + f),
        (dt_ref, 0, None),
    )
    for c, (k_ref, _, row, frames, _) in enumerate(chunks):
        rows = slice(c * f, (c + 1) * f)
        cols = slice(frames[0] * f, (frames[-1] + 1) * f)
        weights = e_scr[rows, cols]
        dscores = (weights.astype(jnp.float32) * (dp_scr[rows, cols] - delta_both[:, cols])).astype(jnp.bfloat16)
        value_term = dot(weights, g_both[cols], NN)
        key_term = dot(dscores, q_both[cols], NN)
        key = k_ref[row:row + f, :]
        for frame in frames:
            part = slice(frame * f - cols.start, (frame + 1) * f - cols.start)
            dq_parts[frame] = dq_parts[frame] + dot(key, dscores[:, part], TN)
        out_ref, at, value_at = outs[c]
        if out_ref is dko_ref:
            dko_ref[at:at + f, :] = key_term
            dvo_ref[at:at + f, :] = value_term
        elif out_ref is dt_ref:
            dt_ref[0, :, :] = key_term.astype(jnp.bfloat16)
            dt_ref[1, :, :] = value_term.astype(jnp.bfloat16)
        else:
            out_ref[at:at + f, :] = key_term.astype(jnp.bfloat16)
            out_ref[value_at:value_at + f, :] = value_term.astype(jnp.bfloat16)
    for frame in range(2):
        cols = slice(frame * f, (frame + 1) * f)
        query_grad = jnp.transpose(dq_parts[frame] * (inv_both[:, cols] * SCALE))
        dq_ref[cols, :] = unrotate(query_grad, cos_ref[cols, :], sin_ref[cols, :]).astype(jnp.bfloat16)


def attend(bias, cosine, sine, query, grad, key, value, left, right, text, before, first, heads):
    tok, width = query.shape
    txt = text.shape[0]
    all_heads = width // D_HEAD
    wide = heads * D_HEAD
    whole = lambda shape: pl.BlockSpec(shape, lambda h: (0, 0))
    here = pl.BlockSpec((tok, D_HEAD), lambda h: (0, first + h))
    upper = pl.BlockSpec((tok, D_HEAD), lambda h: (0, h))
    lower = pl.BlockSpec((tok, D_HEAD), lambda h: (1, h))
    text_k = pl.BlockSpec((txt, D_HEAD), lambda h: (0, first + h))
    text_v = pl.BlockSpec((txt, D_HEAD), lambda h: (0, all_heads + first + h))
    both = pl.BlockSpec((2 * tok, D_HEAD), lambda h: (0, h))
    in_specs = [whole(bias.shape), whole(cosine.shape), whole(sine.shape), here, here, here, here,
                upper, lower, upper, lower, text_k, text_v]
    operands = [bias, cosine, sine, query, grad, key, value, left, left, right, right, text, text]
    aliases = {}
    if before is not None:
        in_specs.append(pl.BlockSpec(memory_space=pl.ANY))
        operands.append(before)
        aliases = {len(operands) - 1: 0}
    keys = 3 * tok + txt
    pairs = tok * (5 * FRAME + txt) * heads
    return pl.pallas_call(
        functools.partial(attend_body, aliased=before is not None),
        grid=(heads,),
        in_specs=in_specs,
        out_specs=[here, upper, upper, both, both, pl.BlockSpec((2, txt, D_HEAD), lambda h: (0, 0, h))],
        out_shape=[
            jax.ShapeDtypeStruct((tok, width), jnp.bfloat16),
            jax.ShapeDtypeStruct((tok, wide), jnp.float32),
            jax.ShapeDtypeStruct((tok, wide), jnp.float32),
            jax.ShapeDtypeStruct((2 * tok, wide), jnp.bfloat16),
            jax.ShapeDtypeStruct((2 * tok, wide), jnp.bfloat16),
            jax.ShapeDtypeStruct((2, txt, wide), jnp.bfloat16),
        ],
        scratch_shapes=[
            pltpu.VMEM((keys, tok), jnp.float32),
            pltpu.VMEM((keys, tok), jnp.float32),
            pltpu.VMEM((keys, tok), jnp.bfloat16),
        ],
        input_output_aliases=aliases,
        compiler_params=pltpu.CompilerParams(vmem_limit_bytes=28 * 2**20),
        cost_estimate=pl.CostEstimate(flops=20 * pairs * D_HEAD, bytes_accessed=20 * tok * wide, transcendentals=pairs),
        name="attend",
    )(*operands)


def finish_body(*refs, aliased):
    cos_ref, sin_ref, dk_ref, dv_ref, lk_ref, lv_ref, rk_ref, rv_ref = refs[:8]
    key_ref, value_ref = refs[8 + (2 if aliased else 0):]
    up = lambda ref: ref[...].astype(jnp.float32)
    key_grad = dk_ref[...] + up(lk_ref) + up(rk_ref)
    key_ref[...] = unrotate(key_grad, cos_ref[...], sin_ref[...]).astype(jnp.bfloat16)
    value_ref[...] = (dv_ref[...] + up(lv_ref) + up(rv_ref)).astype(jnp.bfloat16)


def finish(cosine, sine, key_own, value_own, left_back, right_back, before, first, width):
    tok, wide = key_own.shape
    heads = wide // D_HEAD
    whole = pl.BlockSpec((tok, D_HEAD), lambda h: (0, 0))
    upper = pl.BlockSpec((tok, D_HEAD), lambda h: (0, h))
    lower = pl.BlockSpec((tok, D_HEAD), lambda h: (1, h))
    here = pl.BlockSpec((tok, D_HEAD), lambda h: (0, first + h))
    in_specs = [whole, whole, upper, upper, upper, lower, upper, lower]
    operands = [cosine, sine, key_own, value_own, left_back, left_back, right_back, right_back]
    aliases = {}
    if before is not None:
        in_specs += [pl.BlockSpec(memory_space=pl.ANY)] * 2
        operands += list(before)
        aliases = {8: 0, 9: 1}
    return pl.pallas_call(
        functools.partial(finish_body, aliased=before is not None),
        grid=(heads,),
        in_specs=in_specs,
        out_specs=[here, here],
        out_shape=[jax.ShapeDtypeStruct((tok, width), jnp.bfloat16)] * 2,
        input_output_aliases=aliases,
        compiler_params=pltpu.CompilerParams(vmem_limit_bytes=12 * 2**20),
        cost_estimate=pl.CostEstimate(flops=10 * tok * wide, bytes_accessed=20 * tok * wide, transcendentals=0),
        name="finish",
    )(*operands)


def shards(query_rot, key_rot, value, grad_out, text_key, text_value, positions, tile_mask):
    tok, width = query_rot.shape
    head_count = width // D_HEAD
    heads = head_count // GROUPS
    wide = heads * D_HEAD
    tiles = tok // TILE
    ctx_size = lax.axis_size("ctx")
    ctx_index = lax.axis_index("ctx")
    text_own = jnp.concatenate([text_key, text_value], axis=1)
    text = lax.all_to_all(jnp.tile(text_own, (ctx_size, 1)), "ctx", 0, 0, tiled=True)
    lefts, rights = [], []
    for group in range(GROUPS):
        cols = slice(group * wide, (group + 1) * wide)
        pair = jnp.concatenate([key_rot[:, cols], value[:, cols]], axis=0)
        lefts.append(shifted(pair, "ctx", 1))
        rights.append(shifted(pair, "ctx", -1))
    padded = jnp.pad(tile_mask, ((0, 0), (tiles, tiles)))
    block = lax.dynamic_slice(padded, (ctx_index * tiles, ctx_index * tiles), (tiles, 3 * tiles))
    bias = jnp.where(jnp.repeat(block.T > 0, TILE, axis=1), 0.0, BLOCKED).astype(jnp.float32)
    cosine, sine = rope_tables(positions)
    query_grad, outs, texts = None, [], []
    for group in range(GROUPS):
        query_grad, key_own, value_own, to_left, to_right, text_part = attend(
            bias, cosine, sine, query_rot, grad_out, key_rot, value, lefts[group], rights[group], text,
            query_grad, group * heads, heads)
        outs.append((key_own, value_own, shifted(to_right, "ctx", 1), shifted(to_left, "ctx", -1)))
        texts.append(lax.all_to_all(text_part, "ctx", 1, 1, tiled=True))
    done = None
    for group in range(GROUPS):
        done = finish(cosine, sine, *outs[group], done, group * heads, width)
    sums = [
        part.reshape(2, ctx_size, -1, wide).astype(jnp.float32).sum(axis=1).astype(jnp.bfloat16)
        for part in texts
    ]
    text_grads = jnp.concatenate(sums, axis=2)
    return query_grad, done[0], done[1], text_grads[0], text_grads[1]


def solution(mesh):
    spread = P("ctx", "tp")
    return jax.shard_map(
        shards,
        mesh=mesh,
        in_specs=(spread,) * 6 + (P(None, "ctx"), P()),
        out_specs=(spread,) * 5,
        check_vma=False,
    )
```

time: 787 us -> 162 us (0.21); the launches traced: 772 us -> 159 us
  waiting for transfers between devices: 382 us -> 38.3 us
  blocking collectives: 160 us -> 0 us
  matrix products: 133 us -> 0 us
  starting transfers between devices: 32.9 us -> 64.5 us
  Pallas kernels: 0 us -> 28.7 us
  between operations: 16.4 us -> 0.98 us
  other arithmetic: 21.4 us -> 6.28 us
    unnamed x4 -> x0, waiting for transfers between devices: 381 us -> none
    all_gather x2 -> x0, blocking collectives: 160 us -> none  [the longest x1 88.8 us: shards(): lax.all_gather(text_key, 'ctx', axis=0, tiled=True)]
    dot_general x144 -> x0, matrix products: 133 us -> none  [the longest x24 32.9 us: scores_of(): jnp.einsum('qd,kd->qk', query_head, key_head, preferred_element_type=jnp....]
    all_to_all x0 -> x3, waiting for transfers between devices: none -> 38.3 us  [the longest x1 21.2 us: shards(): lax.all_to_all(jnp.tile(text_own, (ctx_size, 1)), 'ctx', 0, 0, tiled=True)]
    all_to_all x0 -> x3, starting transfers between devices: none -> 31.4 us  [the longest x2 19.5 us: shards(): texts.append(lax.all_to_all(text_part, 'ctx', 1, 1, tiled=True))]
    pallas_call x0 -> x4, Pallas kernels: none -> 28.7 us  [the longest x2 24.3 us: attend(): pl.pallas_call(functools.partial(attend_body, aliased=before is not None)...]
    another operation x2 -> x0, other arithmetic: 7.89 us -> none
    unnamed x190 -> x50, local copies, waits for them, and re-layouts: 21.1 us -> 15.8 us
  transfers between devices with their start and end apart: 10 -> 11, of which waited for: 3 -> 2; matrix products, arithmetic and copies ran while one was open for 18% -> 6% of each run, Pallas kernels for 0% -> 17%
where the time goes in v1:
time: 162 us; the launch traced here: 159 us
  starting transfers between devices  64.5 us (40%)
  waiting for transfers between devices  38.3 us (24%)
  Pallas kernels  28.7 us (18%)
  local copies, waits for them, and re-layouts  20.7 us (13%)
  other arithmetic  6.28 us (4%)
    ppermute x8, starting transfers between devices, shifted(): return lax.ppermute(block, axis, route)  33.2 us
    pallas_call x2, Pallas kernels, attend(): pl.pallas_call(functools.partial(attend_body, aliased=before is not None)...  24.3 us
    all_to_all x1, waiting for transfers between devices, shards(): lax.all_to_all(jnp.tile(text_own, (ctx_size, 1)), 'ctx', 0, 0, tiled=True)  21.2 us
    all_to_all x2, starting transfers between devices, shards(): texts.append(lax.all_to_all(text_part, 'ctx', 1, 1, tiled=True))  19.5 us
    all_to_all x2, waiting for transfers between devices, shards(): texts.append(lax.all_to_all(text_part, 'ctx', 1, 1, tiled=True))  17.1 us
    unnamed x50, local copies, waits for them, and re-layouts  15.8 us
    all_to_all x1, starting transfers between devices, shards(): lax.all_to_all(jnp.tile(text_own, (ctx_size, 1)), 'ctx', 0, 0, tiled=True)  11.9 us
    pallas_call x2, Pallas kernels, finish(): pl.pallas_call(functools.partial(finish_body, aliased=before is not None)...  4.34 us
  transfers between devices with their start and end apart: 11, of which 2 were waited for; matrix products, arithmetic and copies ran while one was open for 6% of the time, Pallas kernels for 17%

profile of v1, /device:TPU:15, one launch (start us, length us, event | category | flops | bytes accessed | tf_op | source)
XLA Modules:
  0.0 159.5 jit_solution(3924799804114814306)
XLA Ops:
  0.6 1.5 fusion.9
  2.1 1.0 pad_maximum_fusion
  3.1 2.4 %collective-permute-start.1 = (bf16[1024,384]{1,0:T(8,128)(2,1)}, bf16[1024,384]{1,0:T(8,128)(2,1)}, u32[]{:S(2)}, u32[]{:S(2)}) collective-permute-start(bf16[1024,384]{1,0:T(8,128)(2,1)} %pad_maximum_fusion), channel_id=1, source_target_pairs={{4,0},{8,4},{12,8},{16,12},{20,16},{24,20},{28,24},{32,28},{36,32}... | collective-permute-start | bytes 2359304 | tf_op jit(solution)/shard_map/ppermute | solution.py:28
  5.6 6.4 %collective-permute-start = (bf16[1024,384]{1,0:T(8,128)(2,1)}, bf16[1024,384]{1,0:T(8,128)(2,1)}, u32[]{:S(2)}, u32[]{:S(2)}) collective-permute-start(bf16[1024,384]{1,0:T(8,128)(2,1)} %pad_maximum_fusion), channel_id=1, source_target_pairs={{0,4},{4,8},{8,12},{12,16},{16,20},{20,24},{24,28},{28,32},{32,36}... | collective-permute-start | bytes 2359304 | tf_op jit(solution)/shard_map/ppermute | solution.py:28
  12.0 0.0 copy-start.21
  12.0 1.0 pad_maximum_fusion.1
  13.0 1.9 %collective-permute-start.3 = (bf16[1024,384]{1,0:T(8,128)(2,1)}, bf16[1024,384]{1,0:T(8,128)(2,1)}, u32[]{:S(2)}, u32[]{:S(2)}) collective-permute-start(bf16[1024,384]{1,0:T(8,128)(2,1)} %pad_maximum_fusion.1), channel_id=1, source_target_pairs={{4,0},{8,4},{12,8},{16,12},{20,16},{24,20},{28,24},{32,28},{36,32}... | collective-permute-start | bytes 2359304 | tf_op jit(solution)/shard_map/ppermute | solution.py:28
  14.9 7.0 %collective-permute-start.2 = (bf16[1024,384]{1,0:T(8,128)(2,1)}, bf16[1024,384]{1,0:T(8,128)(2,1)}, u32[]{:S(2)}, u32[]{:S(2)}) collective-permute-start(bf16[1024,384]{1,0:T(8,128)(2,1)} %pad_maximum_fusion.1), channel_id=1, source_target_pairs={{0,4},{4,8},{8,12},{12,16},{16,20},{20,24},{24,28},{28,32},{32,36}... | collective-permute-start | bytes 2359304 | tf_op jit(solution)/shard_map/ppermute | solution.py:28
  21.9 0.9 tile.2
  22.9 11.9 %all-to-all-start = ((bf16[32,8,1536]{2,1,0:T(8,128)(2,1)}), bf16[32,8,1536]{2,1,0:T(8,128)(2,1)S(1)}, u32[]{:S(2)}, u32[]{:S(2)}) async-start(bf16[32,8,1536]{2,1,0:T(8,128)(2,1)} %tile.2), calls=%async_computation | async-start | bytes 1572864 | tf_op jit(solution)/shard_map/all_to_all | solution.py:246
  34.8 0.1 select_bitcast_fusion
  34.9 0.1 copy.23
  35.0 0.1 broadcast_in_dim.28
  35.1 0.1 broadcast_multiply_fusion.2
  35.3 0.2 broadcast_multiply_fusion.1
  35.5 1.2 negate_select_fusion
  36.7 21.2 %all-to-all-done = bf16[32,8,1536]{2,1,0:T(8,128)(2,1)S(1)} async-done(((bf16[32,8,1536]{2,1,0:T(8,128)(2,1)}), bf16[32,8,1536]{2,1,0:T(8,128)(2,1)S(1)}, u32[]{:S(2)}, u32[]{:S(2)}) %all-to-all-start) | async-done | bytes 786464 | tf_op jit(solution)/shard_map/all_to_all | solution.py:246
  57.9 1.1 copy-done.14
  59.1 1.1 copy-done.16
  60.2 12.2 %attend.2 = (bf16[512,768]{1,0:T(8,128)(2,1)}, f32[512,384]{1,0:T(8,128)S(1)}, f32[512,384]{1,0:T(8,128)S(1)}, bf16[1024,384]{1,0:T(8,128)(2,1)S(1)}, bf16[1024,...) custom-call(f32[12,512]{1,0:T(8,128)S(1)} %bitcast.21, f32[512,128]{1,0:T(8,128)S(1)} %get-tuple-element.42.refs_1_.refs_0_, ...), custom_call_target="tpu_custom_call" | custom-call | flops 6039797760 | bytes 3932160 | tf_op jit(solution)/shard_map/attend/pallas_call | solution.py:176
  72.4 0.9 copy-done.2
  73.3 0.9 copy-done.4
  74.2 0.9 copy-done.18
  75.1 1.2 copy.24
  76.2 10.3 %all-to-all-start.1 = ((bf16[2,256,384]{2,0,1:T(2,128)(2,1)}), bf16[2,256,384]{2,0,1:T(2,128)(2,1)}, u32[]{:S(2)}, u32[]{:S(2)}) async-start(bf16[2,256,384]{2,0,1:T(2,128)(2,1)} %copy.24), calls=%async_computation.1 | async-start | bytes 786432 | tf_op jit(solution)/shard_map/all_to_all | solution.py:263
  86.5 4.6 %collective-permute-start.6 = (bf16[1024,384]{1,0:T(8,128)(2,1)}, bf16[1024,384]{1,0:T(8,128)(2,1)S(1)}, u32[]{:S(2)}, u32[]{:S(2)}) collective-permute-start(bf16[1024,384]{1,0:T(8,128)(2,1)} %get-tuple-element.29), channel_id=1, source_target_pairs={{0,4},{4,8},{8,12},{12,16},{16,20},{20,24},{24,28},{28,32},{32,36}... | collective-permute-start | bytes 2359304 | tf_op jit(solution)/shard_map/ppermute | solution.py:28
  91.1 1.9 %collective-permute-start.7 = (bf16[1024,384]{1,0:T(8,128)(2,1)}, bf16[1024,384]{1,0:T(8,128)(2,1)S(1)}, u32[]{:S(2)}, u32[]{:S(2)}) collective-permute-start(bf16[1024,384]{1,0:T(8,128)(2,1)} %copy-done.18), channel_id=1, source_target_pairs={{4,0},{8,4},{12,8},{16,12},{20,16},{24,20},{28,24},{32,28},{36,32}... | collective-permute-start | bytes 2359304 | tf_op jit(solution)/shard_map/ppermute | solution.py:28
  93.1 1.1 copy-done.7
  94.2 1.1 copy-done.9
  95.3 1.1 copy-done.15
  96.5 1.1 copy-done.17
  97.6 12.2 %attend.3 = (bf16[512,768]{1,0:T(8,128)(2,1)}, f32[512,384]{1,0:T(8,128)S(1)}, f32[512,384]{1,0:T(8,128)S(1)}, bf16[1024,384]{1,0:T(8,128)(2,1)}, bf16[1024,384]...) custom-call(f32[12,512]{1,0:T(8,128)S(1)} %bitcast.22, ...), custom_call_target="tpu_custom_call", output_to_operand_aliasing={{0}: (13, {})} | custom-call | flops 6039797760 | bytes 3932160 | tf_op jit(solution)/shard_map/attend/pallas_call | solution.py:176
  109.8 0.9 copy-done.10
  110.7 0.9 copy-done.12
  111.6 7.0 %collective-permute-start.4 = (bf16[1024,384]{1,0:T(8,128)(2,1)}, bf16[1024,384]{1,0:T(8,128)(2,1)S(1)}, u32[]{:S(2)}, u32[]{:S(2)}) collective-permute-start(bf16[1024,384]{1,0:T(8,128)(2,1)} %get-tuple-element.25), channel_id=1, source_target_pairs={{0,4},{4,8},{8,12},{12,16},{16,20},{20,24},{24,28},{28,32},{32,36}... | collective-permute-start | bytes 2359304 | tf_op jit(solution)/shard_map/ppermute | solution.py:28
  118.5 1.9 %collective-permute-start.5 = (bf16[1024,384]{1,0:T(8,128)(2,1)}, bf16[1024,384]{1,0:T(8,128)(2,1)S(1)}, u32[]{:S(2)}, u32[]{:S(2)}) collective-permute-start(bf16[1024,384]{1,0:T(8,128)(2,1)} %get-tuple-element.26), channel_id=1, source_target_pairs={{4,0},{8,4},{12,8},{16,12},{20,16},{24,20},{28,24},{32,28},{36,32}... | collective-permute-start | bytes 2359304 | tf_op jit(solution)/shard_map/ppermute | solution.py:28
  120.5 1.2 copy.25
  121.6 9.2 %all-to-all-start.2 = ((bf16[2,256,384]{2,0,1:T(2,128)(2,1)}), bf16[2,256,384]{2,0,1:T(2,128)(2,1)}, u32[]{:S(2)}, u32[]{:S(2)}) async-start(bf16[2,256,384]{2,0,1:T(2,128)(2,1)} %copy.25), calls=%async_computation.2 | async-start | bytes 786432 | tf_op jit(solution)/shard_map/all_to_all | solution.py:263
  130.9 1.3 reduce_sum.24
  132.2 17.1 %all-to-all-done.2 = bf16[2,256,384]{2,0,1:T(2,128)(2,1)} async-done(((bf16[2,256,384]{2,0,1:T(2,128)(2,1)}), bf16[2,256,384]{2,0,1:T(2,128)(2,1)}, u32[]{:S(2)}, u32[]{:S(2)}) %all-to-all-start.2) | async-done | bytes 393248 | tf_op jit(solution)/shard_map/all_to_all | solution.py:263
  149.3 1.3 reduce_sum.25
  150.6 0.6 copy.31
  151.3 0.6 copy.32
  151.9 0.9 copy-done.1
  152.8 1.1 copy-done.3
  154.0 1.1 copy-done.5
  155.1 2.1 %finish.2 = (bf16[512,768]{1,0:T(8,128)(2,1)}, bf16[512,768]{1,0:T(8,128)(2,1)}) custom-call(f32[512,128]{1,0:T(8,128)S(1)} %copy-done.1, f32[512,128]{1,0:T(8,128)S(1)} %get-tuple-element.41.refs_2_.refs_1_, f32[512,384]{1,0:T(8,128)S(1)} %copy-done.3, f32[512,384]{1,0:T(8,128)S(1)} %copy-done.5, ...), custom_call_target="tpu_custom_call" | custom-call | flops 1966080 | bytes 3932160 | tf_op jit(solution)/shard_map/finish/pallas_call | solution.py:224
  157.3 2.2 %finish.3 = (bf16[512,768]{1,0:T(8,128)(2,1)}, bf16[512,768]{1,0:T(8,128)(2,1)}) custom-call(f32[512,128]{1,0:T(8,128)S(1)} %copy-done.1, f32[512,128]{1,0:T(8,128)S(1)} %get-tuple-element.41.refs_2_.refs_1_, f32[512,384]{1,0:T(8,128)S(1)} %copy-done.11, f32[512,384]{1,0:T(8,128)S(1)} %copy-done.13, ...), custom_call_target="tpu_custom_call", output_to_operand_aliasing={{0}: (8, {}), {1}: (9, {})} | custom-call | flops 1966080 | bytes 3932160 | tf_op jit(solution)/shard_map/finish/pallas_call | solution.py:224
  (49 shorter events, 0.2 us)
Async XLA Ops:
  3.1 89.9 %collective-permute-start.1 = (bf16[1024,384]{1,0:T(8,128)(2,1)}, bf16[1024,384]{1,0:T(8,128)(2,1)}, u32[]{:S(2)}, u32[]{:S(2)}) collective-permute-start(bf16[1024,384]{1,0:T(8,128)(2,1)} %pad_maximum_fusion), channel_id=1, source_target_pairs={{4,0},{8,4},{12,8},{16,12},{20,16},{24,20},{28,24},{32,28},{36,32}... | collective-permute-start | bytes 2359304 | tf_op jit(solution)/shard_map/ppermute | solution.py:28
  5.6 87.5 %collective-permute-start = (bf16[1024,384]{1,0:T(8,128)(2,1)}, bf16[1024,384]{1,0:T(8,128)(2,1)}, u32[]{:S(2)}, u32[]{:S(2)}) collective-permute-start(bf16[1024,384]{1,0:T(8,128)(2,1)} %pad_maximum_fusion), channel_id=1, source_target_pairs={{0,4},{4,8},{8,12},{12,16},{16,20},{20,24},{24,28},{28,32},{32,36}... | collective-permute-start | bytes 2359304 | tf_op jit(solution)/shard_map/ppermute | solution.py:28
  12.0 9.9 %copy-start.20 = (bf16[8,768]{1,0:T(8,128)(2,1)S(1)}, bf16[8,768]{1,0:T(8,128)(2,1)}, u32[]{:S(2)}) copy-start(bf16[8,768]{1,0:T(8,128)(2,1)} %param.13) | copy-start | bytes 36868
  12.0 9.9 %copy-start.21 = (bf16[8,768]{1,0:T(8,128)(2,1)S(1)}, bf16[8,768]{1,0:T(8,128)(2,1)}, u32[]{:S(2)}) copy-start(bf16[8,768]{1,0:T(8,128)(2,1)} %param.12) | copy-start | bytes 36868
  13.0 44.9 %collective-permute-start.3 = (bf16[1024,384]{1,0:T(8,128)(2,1)}, bf16[1024,384]{1,0:T(8,128)(2,1)}, u32[]{:S(2)}, u32[]{:S(2)}) collective-permute-start(bf16[1024,384]{1,0:T(8,128)(2,1)} %pad_maximum_fusion.1), channel_id=1, source_target_pairs={{4,0},{8,4},{12,8},{16,12},{20,16},{24,20},{28,24},{32,28},{36,32}... | collective-permute-start | bytes 2359304 | tf_op jit(solution)/shard_map/ppermute | solution.py:28
  14.9 43.0 %collective-permute-start.2 = (bf16[1024,384]{1,0:T(8,128)(2,1)}, bf16[1024,384]{1,0:T(8,128)(2,1)}, u32[]{:S(2)}, u32[]{:S(2)}) collective-permute-start(bf16[1024,384]{1,0:T(8,128)(2,1)} %pad_maximum_fusion.1), channel_id=1, source_target_pairs={{0,4},{4,8},{8,12},{12,16},{16,20},{20,24},{24,28},{28,32},{32,36}... | collective-permute-start | bytes 2359304 | tf_op jit(solution)/shard_map/ppermute | solution.py:28
  22.9 11.9 %copy-start.22 = (s32[3,512]{1,0:T(4,128)S(1)}, s32[3,512]{1,0:T(4,128)}, u32[]{:S(2)}) copy-start(s32[3,512]{1,0:T(4,128)} %param.14) | copy-start | bytes 18436
  22.9 12.0 %copy-start.19 = (s32[128,128]{1,0:T(8,128)S(1)}, s32[128,128]{1,0:T(8,128)}, u32[]{:S(2)}) copy-start(s32[128,128]{1,0:T(8,128)} %param.15) | copy-start | bytes 196612
  22.9 35.0 %all-to-all-start = ((bf16[32,8,1536]{2,1,0:T(8,128)(2,1)}), bf16[32,8,1536]{2,1,0:T(8,128)(2,1)S(1)}, u32[]{:S(2)}, u32[]{:S(2)}) async-start(bf16[32,8,1536]{2,1,0:T(8,128)(2,1)} %tile.2), calls=%async_computation | async-start | bytes 1572864 | tf_op jit(solution)/shard_map/all_to_all | solution.py:246
  35.3 22.7 %copy-start.8 = (bf16[512,768]{1,0:T(8,128)(2,1)S(1)}, bf16[512,768]{1,0:T(8,128)(2,1)}, u32[]{:S(2)}) copy-start(bf16[512,768]{1,0:T(8,128)(2,1)} %refs_6_.3) | copy-start | bytes 2359300
  35.5 22.4 %copy-start.6 = (bf16[512,768]{1,0:T(8,128)(2,1)S(1)}, bf16[512,768]{1,0:T(8,128)(2,1)}, u32[]{:S(2)}) copy-start(bf16[512,768]{1,0:T(8,128)(2,1)} %refs_5_.3) | copy-start | bytes 2359300
  36.7 56.4 %copy-start = (f32[512,128]{1,0:T(8,128)}, f32[512,128]{1,0:T(8,128)S(1)}, u32[]{:S(2)}) copy-start(f32[512,128]{1,0:T(8,128)S(1)} %get-tuple-element.42.refs_1_.refs_0_) | copy-start | bytes 786436
  57.9 1.1 copy-start.14
  59.1 1.1 copy-start.16
  72.4 0.9 copy-start.2
  73.3 0.9 copy-start.4
  74.2 0.9 copy-start.18
  76.2 45.4 %all-to-all-start.1 = ((bf16[2,256,384]{2,0,1:T(2,128)(2,1)}), bf16[2,256,384]{2,0,1:T(2,128)(2,1)}, u32[]{:S(2)}, u32[]{:S(2)}) async-start(bf16[2,256,384]{2,0,1:T(2,128)(2,1)} %copy.24), calls=%async_computation.1 | async-start | bytes 786432 | tf_op jit(solution)/shard_map/all_to_all | solution.py:263
  86.5 65.3 %collective-permute-start.6 = (bf16[1024,384]{1,0:T(8,128)(2,1)}, bf16[1024,384]{1,0:T(8,128)(2,1)S(1)}, u32[]{:S(2)}, u32[]{:S(2)}) collective-permute-start(bf16[1024,384]{1,0:T(8,128)(2,1)} %get-tuple-element.29), channel_id=1, source_target_pairs={{0,4},{4,8},{8,12},{12,16},{16,20},{20,24},{24,28},{28,32},{32,36}... | collective-permute-start | bytes 2359304 | tf_op jit(solution)/shard_map/ppermute | solution.py:28
  91.1 60.7 %collective-permute-start.7 = (bf16[1024,384]{1,0:T(8,128)(2,1)}, bf16[1024,384]{1,0:T(8,128)(2,1)S(1)}, u32[]{:S(2)}, u32[]{:S(2)}) collective-permute-start(bf16[1024,384]{1,0:T(8,128)(2,1)} %copy-done.18), channel_id=1, source_target_pairs={{4,0},{8,4},{12,8},{16,12},{20,16},{24,20},{28,24},{32,28},{36,32}... | collective-permute-start | bytes 2359304 | tf_op jit(solution)/shard_map/ppermute | solution.py:28
  93.1 1.1 copy-start.7
  94.2 1.1 copy-start.9
  95.3 1.1 copy-start.15
  96.5 1.1 copy-start.17
  109.8 0.9 copy-start.10
  110.7 0.9 copy-start.12
  111.6 45.7 %collective-permute-start.4 = (bf16[1024,384]{1,0:T(8,128)(2,1)}, bf16[1024,384]{1,0:T(8,128)(2,1)S(1)}, u32[]{:S(2)}, u32[]{:S(2)}) collective-permute-start(bf16[1024,384]{1,0:T(8,128)(2,1)} %get-tuple-element.25), channel_id=1, source_target_pairs={{0,4},{4,8},{8,12},{12,16},{16,20},{20,24},{24,28},{28,32},{32,36}... | collective-permute-start | bytes 2359304 | tf_op jit(solution)/shard_map/ppermute | solution.py:28
  118.5 38.7 %collective-permute-start.5 = (bf16[1024,384]{1,0:T(8,128)(2,1)}, bf16[1024,384]{1,0:T(8,128)(2,1)S(1)}, u32[]{:S(2)}, u32[]{:S(2)}) collective-permute-start(bf16[1024,384]{1,0:T(8,128)(2,1)} %get-tuple-element.26), channel_id=1, source_target_pairs={{4,0},{8,4},{12,8},{16,12},{20,16},{24,20},{28,24},{32,28},{36,32}... | collective-permute-start | bytes 2359304 | tf_op jit(solution)/shard_map/ppermute | solution.py:28
  121.6 27.6 %all-to-all-start.2 = ((bf16[2,256,384]{2,0,1:T(2,128)(2,1)}), bf16[2,256,384]{2,0,1:T(2,128)(2,1)}, u32[]{:S(2)}, u32[]{:S(2)}) async-start(bf16[2,256,384]{2,0,1:T(2,128)(2,1)} %copy.25), calls=%async_computation.2 | async-start | bytes 786432 | tf_op jit(solution)/shard_map/all_to_all | solution.py:263
  151.9 1.0 copy-start.1
  152.8 1.1 copy-start.3
  153.9 1.1 copy-start.5
  155.1 2.2 %copy-start.11 = (f32[512,384]{1,0:T(8,128)S(1)}, f32[512,384]{1,0:T(8,128)}, u32[]{:S(2)}) copy-start(f32[512,384]{1,0:T(8,128)} %copy-done.10) | copy-start | bytes 2359300
  155.1 2.2 %copy-start.13 = (f32[512,384]{1,0:T(8,128)S(1)}, f32[512,384]{1,0:T(8,128)}, u32[]{:S(2)}) copy-start(f32[512,384]{1,0:T(8,128)} %copy-done.12) | copy-start | bytes 2359300

commit v2 on v1

--- a/solution.py
+++ b/solution.py
@@ -16,16 +16,34 @@
 SCALE = D_HEAD ** (-0.5)
 EXP2_SCALE = SCALE * math.log2(math.e)
 BLOCKED = 1e30
-GROUPS = 2
+SPLIT = (1, 1)
 NT = (((1,), (1,)), ((), ()))
 NN = (((1,), (0,)), ((), ()))
 TN = (((0,), (0,)), ((), ()))
 
 
-def shifted(block, axis, distance):
-    devices = range(lax.axis_size(axis))
-    route = [(i - distance, i) for i in devices if i - distance in devices]
+def exchange(block, axis, first):
+    size = lax.axis_size(axis)
+    route = []
+    for low in range(first, size - 1, 2):
+        route += [(low, low + 1), (low + 1, low)]
     return lax.ppermute(block, axis, route)
+
+
+def text_groups(size):
+    run = min(8, size)
+    near = [list(range(start, start + run)) for start in range(0, size, run)]
+    far = [list(range(place, size, run)) for place in range(run)]
+    return near, far
+
+
+def swap(rows, groups):
+    return lax.all_to_all(rows, "ctx", 0, 0, axis_index_groups=groups, tiled=True)
+
+
+def part_sum(rows, parts):
+    terms = rows.reshape(parts, -1, rows.shape[1]).astype(jnp.float32)
+    return terms.sum(axis=0).astype(jnp.bfloat16)
 
 
 def rope_tables(positions):
@@ -59,10 +77,21 @@
     return combine(block.reshape(block.shape[0] // 8, 8, block.shape[1]), axis=0)
 
 
+def by_place(rows):
+    own, run = 8, 8
+    tiles = rows.reshape(-1, run, own, rows.shape[1])
+    return jnp.concatenate([tiles[r, place] for place in range(run) for r in range(tiles.shape[0])], axis=0)
+
+
 def attend_body(*refs, aliased):
-    (bias_ref, cos_ref, sin_ref, q_ref, g_ref, ko_ref, vo_ref, kl_ref, vl_ref, kr_ref, vr_ref, tk_ref, tv_ref) = refs[:13]
-    refs = refs[13 + (1 if aliased else 0):]
-    dq_ref, dko_ref, dvo_ref, dl_ref, dr_ref, dt_ref, s_scr, dp_scr, e_scr = refs
+    (place_ref, bias_ref, cos_ref, sin_ref, q_ref, g_ref, ko_ref, vo_ref, ka_ref, va_ref, kb_ref, vb_ref, tk_ref,
+     tv_ref) = refs[:14]
+    refs = refs[14 + (1 if aliased else 0):]
+    dq_ref, dko_ref, dvo_ref, da_ref, db_ref, dt_ref, s_scr, dp_scr, e_scr, kl_ref, vl_ref, kr_ref, vr_ref = refs
+    even = place_ref[0] % 2 == 0
+    for left_ref, right_ref, a_ref, b_ref in ((kl_ref, kr_ref, ka_ref, kb_ref), (vl_ref, vr_ref, va_ref, vb_ref)):
+        left_ref[...] = jnp.where(even, b_ref[...], a_ref[...])
+        right_ref[...] = jnp.where(even, a_ref[...], b_ref[...])
     tok = q_ref.shape[0]
     f = FRAME
     chunks = (
@@ -118,12 +147,7 @@
     delta_both = jnp.concatenate(delta_rows, axis=1)
     inv_both = jnp.concatenate(inv_rows, axis=1)
     dq_parts = [jnp.zeros((D_HEAD, f), jnp.float32) for _ in range(2)]
-    outs = (
-        (dl_ref, 0, tok), (dl_ref, f, tok + f),
-        (dko_ref, 0, None), (dko_ref, f, None),
-        (dr_ref, 0, tok), (dr_ref, f, tok + f),
-        (dt_ref, 0, None),
-    )
+    sides = {}
     for c, (k_ref, _, row, frames, _) in enumerate(chunks):
         rows = slice(c * f, (c + 1) * f)
         cols = slice(frames[0] * f, (frames[-1] + 1) * f)
@@ -135,23 +159,29 @@
         for frame in frames:
             part = slice(frame * f - cols.start, (frame + 1) * f - cols.start)
             dq_parts[frame] = dq_parts[frame] + dot(key, dscores[:, part], TN)
-        out_ref, at, value_at = outs[c]
-        if out_ref is dko_ref:
-            dko_ref[at:at + f, :] = key_term
-            dvo_ref[at:at + f, :] = value_term
-        elif out_ref is dt_ref:
-            dt_ref[0, :, :] = key_term.astype(jnp.bfloat16)
-            dt_ref[1, :, :] = value_term.astype(jnp.bfloat16)
+        if k_ref is ko_ref:
+            dko_ref[row:row + f, :] = key_term
+            dvo_ref[row:row + f, :] = value_term
+        elif k_ref is tk_ref:
+            at = pl.multiple_of(pl.program_id(0) * D_HEAD, D_HEAD)
+            value_at = pl.multiple_of(at + dt_ref.shape[1] // 2, D_HEAD)
+            dt_ref[:, pl.ds(at, D_HEAD)] = by_place(key_term).astype(jnp.bfloat16)
+            dt_ref[:, pl.ds(value_at, D_HEAD)] = by_place(value_term).astype(jnp.bfloat16)
         else:
-            out_ref[at:at + f, :] = key_term.astype(jnp.bfloat16)
-            out_ref[value_at:value_at + f, :] = value_term.astype(jnp.bfloat16)
+            sides[k_ref is kr_ref, row] = key_term.astype(jnp.bfloat16), value_term.astype(jnp.bfloat16)
+            if k_ref is kr_ref:
+                for kind in range(2):
+                    to_left, to_right = sides[False, row][kind], sides[True, row][kind]
+                    rows = slice(kind * tok + row, kind * tok + row + f)
+                    da_ref[rows, :] = jnp.where(even, to_right, to_left)
+                    db_ref[rows, :] = jnp.where(even, to_left, to_right)
     for frame in range(2):
         cols = slice(frame * f, (frame + 1) * f)
         query_grad = jnp.transpose(dq_parts[frame] * (inv_both[:, cols] * SCALE))
         dq_ref[cols, :] = unrotate(query_grad, cos_ref[cols, :], sin_ref[cols, :]).astype(jnp.bfloat16)
 
 
-def attend(bias, cosine, sine, query, grad, key, value, left, right, text, before, first, heads):
+def attend(place, bias, cosine, sine, query, grad, key, value, left, right, text, before, first, heads):
     tok, width = query.shape
     txt = text.shape[0]
     all_heads = width // D_HEAD
@@ -163,9 +193,9 @@
     text_k = pl.BlockSpec((txt, D_HEAD), lambda h: (0, first + h))
     text_v = pl.BlockSpec((txt, D_HEAD), lambda h: (0, all_heads + first + h))
     both = pl.BlockSpec((2 * tok, D_HEAD), lambda h: (0, h))
-    in_specs = [whole(bias.shape), whole(cosine.shape), whole(sine.shape), here, here, here, here,
+    in_specs = [pl.BlockSpec(memory_space=pltpu.SMEM), whole(bias.shape), whole(cosine.shape), whole(sine.shape), here, here, here, here,
                 upper, lower, upper, lower, text_k, text_v]
-    operands = [bias, cosine, sine, query, grad, key, value, left, left, right, right, text, text]
+    operands = [place, bias, cosine, sine, query, grad, key, value, left, left, right, right, text, text]
     aliases = {}
     if before is not None:
         in_specs.append(pl.BlockSpec(memory_space=pl.ANY))
@@ -177,45 +207,48 @@
         functools.partial(attend_body, aliased=before is not None),
         grid=(heads,),
         in_specs=in_specs,
-        out_specs=[here, upper, upper, both, both, pl.BlockSpec((2, txt, D_HEAD), lambda h: (0, 0, h))],
+        out_specs=[here, upper, upper, both, both, whole((txt, 2 * wide))],
         out_shape=[
             jax.ShapeDtypeStruct((tok, width), jnp.bfloat16),
             jax.ShapeDtypeStruct((tok, wide), jnp.float32),
             jax.ShapeDtypeStruct((tok, wide), jnp.float32),
             jax.ShapeDtypeStruct((2 * tok, wide), jnp.bfloat16),
             jax.ShapeDtypeStruct((2 * tok, wide), jnp.bfloat16),
-            jax.ShapeDtypeStruct((2, txt, wide), jnp.bfloat16),
+            jax.ShapeDtypeStruct((txt, 2 * wide), jnp.bfloat16),
         ],
         scratch_shapes=[
             pltpu.VMEM((keys, tok), jnp.float32),
             pltpu.VMEM((keys, tok), jnp.float32),
             pltpu.VMEM((keys, tok), jnp.bfloat16),
-        ],
+        ] + [pltpu.VMEM((tok, D_HEAD), jnp.bfloat16)] * 4,
         input_output_aliases=aliases,
-        compiler_params=pltpu.CompilerParams(vmem_limit_bytes=28 * 2**20),
-        cost_estimate=pl.CostEstimate(flops=20 * pairs * D_HEAD, bytes_accessed=20 * tok * wide, transcendentals=pairs),
+        compiler_params=pltpu.CompilerParams(vmem_limit_bytes=56 * 2**20),
+        cost_estimate=pl.CostEstimate(flops=pairs, bytes_accessed=tok * wide, transcendentals=0),
         name="attend",
     )(*operands)
 
 
 def finish_body(*refs, aliased):
-    cos_ref, sin_ref, dk_ref, dv_ref, lk_ref, lv_ref, rk_ref, rv_ref = refs[:8]
+    cos_ref, sin_ref, dk_ref, dv_ref, ak_ref, av_ref, bk_ref, bv_ref = refs[:8]
     key_ref, value_ref = refs[8 + (2 if aliased else 0):]
-    up = lambda ref: ref[...].astype(jnp.float32)
-    key_grad = dk_ref[...] + up(lk_ref) + up(rk_ref)
-    key_ref[...] = unrotate(key_grad, cos_ref[...], sin_ref[...]).astype(jnp.bfloat16)
-    value_ref[...] = (dv_ref[...] + up(lv_ref) + up(rv_ref)).astype(jnp.bfloat16)
-
-
-def finish(cosine, sine, key_own, value_own, left_back, right_back, before, first, width):
+    up = lambda ref, cols: ref[:, cols].astype(jnp.float32)
+    cosine, sine = cos_ref[...], sin_ref[...]
+    for head in range(dk_ref.shape[1] // D_HEAD):
+        cols = slice(head * D_HEAD, (head + 1) * D_HEAD)
+        key_grad = dk_ref[:, cols] + up(ak_ref, cols) + up(bk_ref, cols)
+        key_ref[:, cols] = unrotate(key_grad, cosine, sine).astype(jnp.bfloat16)
+        value_ref[:, cols] = (dv_ref[:, cols] + up(av_ref, cols) + up(bv_ref, cols)).astype(jnp.bfloat16)
+
+
+def finish(cosine, sine, key_own, value_own, back_a, back_b, before, first, width):
     tok, wide = key_own.shape
-    heads = wide // D_HEAD
-    whole = pl.BlockSpec((tok, D_HEAD), lambda h: (0, 0))
-    upper = pl.BlockSpec((tok, D_HEAD), lambda h: (0, h))
-    lower = pl.BlockSpec((tok, D_HEAD), lambda h: (1, h))
-    here = pl.BlockSpec((tok, D_HEAD), lambda h: (0, first + h))
-    in_specs = [whole, whole, upper, upper, upper, lower, upper, lower]
-    operands = [cosine, sine, key_own, value_own, left_back, left_back, right_back, right_back]
+    step = tok // 2
+    upper = pl.BlockSpec((step, wide), lambda r: (r, 0))
+    lower = pl.BlockSpec((step, wide), lambda r: (tok // step + r, 0))
+    table = pl.BlockSpec((step, D_HEAD), lambda r: (r, 0))
+    here = pl.BlockSpec((step, wide), lambda r: (r, first * D_HEAD // wide))
+    in_specs = [table, table, upper, upper, upper, lower, upper, lower]
+    operands = [cosine, sine, key_own, value_own, back_a, back_a, back_b, back_b]
     aliases = {}
     if before is not None:
         in_specs += [pl.BlockSpec(memory_space=pl.ANY)] * 2
@@ -223,12 +256,12 @@
         aliases = {8: 0, 9: 1}
     return pl.pallas_call(
         functools.partial(finish_body, aliased=before is not None),
-        grid=(heads,),
+        grid=(tok // step,),
         in_specs=in_specs,
         out_specs=[here, here],
         out_shape=[jax.ShapeDtypeStruct((tok, width), jnp.bfloat16)] * 2,
         input_output_aliases=aliases,
-        compiler_params=pltpu.CompilerParams(vmem_limit_bytes=12 * 2**20),
+        compiler_params=pltpu.CompilerParams(vmem_limit_bytes=56 * 2**20),
         cost_estimate=pl.CostEstimate(flops=10 * tok * wide, bytes_accessed=20 * tok * wide, transcendentals=0),
         name="finish",
     )(*operands)
@@ -237,39 +270,50 @@
 def shards(query_rot, key_rot, value, grad_out, text_key, text_value, positions, tile_mask):
     tok, width = query_rot.shape
     head_count = width // D_HEAD
-    heads = head_count // GROUPS
-    wide = heads * D_HEAD
+    sizes = [head_count * share // sum(SPLIT) for share in SPLIT]
+    firsts = [sum(sizes[:group]) for group in range(len(sizes))]
     tiles = tok // TILE
     ctx_size = lax.axis_size("ctx")
     ctx_index = lax.axis_index("ctx")
     text_own = jnp.concatenate([text_key, text_value], axis=1)
+    near, far = text_groups(ctx_size)
+
+    def halo(keys, values, group):
+        cols = slice(firsts[group] * D_HEAD, (firsts[group] + sizes[group]) * D_HEAD)
+        pair = jnp.concatenate([keys[:, cols], values[:, cols]], axis=0)
+        return exchange(pair, "ctx", 0), exchange(pair, "ctx", 1)
+
+    halos = [halo(key_rot, value, 0)]
     text = lax.all_to_all(jnp.tile(text_own, (ctx_size, 1)), "ctx", 0, 0, tiled=True)
-    lefts, rights = [], []
-    for group in range(GROUPS):
-        cols = slice(group * wide, (group + 1) * wide)
-        pair = jnp.concatenate([key_rot[:, cols], value[:, cols]], axis=0)
-        lefts.append(shifted(pair, "ctx", 1))
-        rights.append(shifted(pair, "ctx", -1))
+    text, keys_later, values_later = lax.optimization_barrier((text, key_rot, value))
+    halos += [halo(keys_later, values_later, group) for group in range(1, len(sizes))]
     padded = jnp.pad(tile_mask, ((0, 0), (tiles, tiles)))
     block = lax.dynamic_slice(padded, (ctx_index * tiles, ctx_index * tiles), (tiles, 3 * tiles))
     bias = jnp.where(jnp.repeat(block.T > 0, TILE, axis=1), 0.0, BLOCKED).astype(jnp.float32)
     cosine, sine = rope_tables(positions)
-    query_grad, outs, texts = None, [], []
-    for group in range(GROUPS):
-        query_grad, key_own, value_own, to_left, to_right, text_part = attend(
-            bias, cosine, sine, query_rot, grad_out, key_rot, value, lefts[group], rights[group], text,
-            query_grad, group * heads, heads)
-        outs.append((key_own, value_own, shifted(to_right, "ctx", 1), shifted(to_left, "ctx", -1)))
-        texts.append(lax.all_to_all(text_part, "ctx", 1, 1, tiled=True))
-    done = None
-    for group in range(GROUPS):
-        done = finish(cosine, sine, *outs[group], done, group * heads, width)
-    sums = [
-        part.reshape(2, ctx_size, -1, wide).astype(jnp.float32).sum(axis=1).astype(jnp.bfloat16)
-        for part in texts
-    ]
-    text_grads = jnp.concatenate(sums, axis=2)
-    return query_grad, done[0], done[1], text_grads[0], text_grads[1]
+    place = jnp.full((1,), ctx_index, jnp.int32)
+    query_grad, waiting, done, near_texts = None, None, None, []
+    for group, (first, heads) in enumerate(zip(firsts, sizes)):
+        query_grad, key_own, value_own, to_even, to_odd, text_part = attend(
+            place, bias, cosine, sine, query_rot, grad_out, key_rot, value, *halos[group], text,
+            query_grad, first, heads)
+        if waiting is not None:
+            sent, ready = waiting[2:], (to_even, to_odd, text_part)
+            sent, (to_even, to_odd, text_part) = lax.optimization_barrier((sent, ready))
+            near_texts.append(sent[2])
+            done = finish(cosine, sine, *waiting[:2], *sent[:2], done, firsts[group - 1], width)
+        waiting = (key_own, value_own, exchange(to_even, "ctx", 0), exchange(to_odd, "ctx", 1), swap(text_part, near))
+    near_texts.append(waiting[4])
+    done = finish(cosine, sine, *waiting[:4], done, firsts[-1], width)
+    near_sums = jnp.concatenate([part_sum(part, len(near[0])) for part in near_texts], axis=1)
+    text_grads = part_sum(swap(near_sums, far), len(far[0]))
+    starts = [2 * first * D_HEAD for first in firsts]
+    text_key_grad, text_value_grad = (
+        jnp.concatenate([text_grads[:, at + k * heads * D_HEAD:at + (k + 1) * heads * D_HEAD]
+                         for at, heads in zip(starts, sizes)], axis=1)
+        for k in range(2)
+    )
+    return query_grad, done[0], done[1], text_key_grad, text_value_grad
 
 
 def solution(mesh):

time: 162 us -> 131 us (0.81); the launches traced: 159 us -> 130 us
  starting transfers between devices: 64.5 us -> 47.8 us
  local copies, waits for them, and re-layouts: 20.7 us -> 6.49 us
  waiting for transfers between devices: 38.3 us -> 34.9 us
  Pallas kernels: 28.7 us -> 31.9 us
  other arithmetic: 6.28 us -> 8.1 us
    unnamed x50 -> x24, local copies, waits for them, and re-layouts: 15.8 us -> 3.75 us
    ppermute x8, starting transfers between devices: 33.2 us -> 21.7 us  [exchange(): return lax.ppermute(block, axis, route)]
    all_to_all x1, starting transfers between devices: 11.9 us -> 7.99 us  [shards(): lax.all_to_all(jnp.tile(text_own, (ctx_size, 1)), 'ctx', 0, 0, tiled=True)]
    all_to_all x1, waiting for transfers between devices: 21.2 us -> 18.9 us  [shards(): lax.all_to_all(jnp.tile(text_own, (ctx_size, 1)), 'ctx', 0, 0, tiled=True)]
    pallas_call x2 -> x0, local copies, waits for them, and re-layouts: 2.32 us -> none  [attend(): pl.pallas_call(functools.partial(attend_body, aliased=before is not None)...]
    pallas_call x2, Pallas kernels: 4.34 us -> 6.1 us  [finish(): pl.pallas_call(functools.partial(finish_body, aliased=before is not None)...]
    all_to_all x2 -> x3, starting transfers between devices: 19.5 us -> 18.1 us  [swap(): lax.all_to_all(rows, 'ctx', 0, 0, axis_index_groups=groups, tiled=True)]
    all_to_all x2 -> x3, waiting for transfers between devices: 17.1 us -> 16 us  [swap(): lax.all_to_all(rows, 'ctx', 0, 0, axis_index_groups=groups, tiled=True)]
  transfers between devices with their start and end apart: 11 -> 12, of which waited for: 2 -> 3; matrix products, arithmetic and copies ran while one was open for 6% -> 7% of each run, Pallas kernels for 17% -> 22%
where the time goes in v2:
time: 131 us; the launch traced here: 130 us
  starting transfers between devices  47.8 us (36%)
  waiting for transfers between devices  34.9 us (27%)
  Pallas kernels  31.9 us (24%)
  other arithmetic  8.1 us (6%)
  local copies, waits for them, and re-layouts  6.49 us (5%)
    pallas_call x2, Pallas kernels, attend(): pl.pallas_call(functools.partial(attend_body, aliased=before is not None)...  25.8 us
    ppermute x8, starting transfers between devices, exchange(): return lax.ppermute(block, axis, route)  21.7 us
    all_to_all x1, waiting for transfers between devices, shards(): lax.all_to_all(jnp.tile(text_own, (ctx_size, 1)), 'ctx', 0, 0, tiled=True)  18.9 us
    all_to_all x3, starting transfers between devices, swap(): lax.all_to_all(rows, 'ctx', 0, 0, axis_index_groups=groups, tiled=True)  18.1 us
    all_to_all x3, waiting for transfers between devices, swap(): lax.all_to_all(rows, 'ctx', 0, 0, axis_index_groups=groups, tiled=True)  16 us
    all_to_all x1, starting transfers between devices, shards(): lax.all_to_all(jnp.tile(text_own, (ctx_size, 1)), 'ctx', 0, 0, tiled=True)  7.99 us
    pallas_call x2, Pallas kernels, finish(): pl.pallas_call(functools.partial(finish_body, aliased=before is not None)...  6.1 us
    unnamed x24, local copies, waits for them, and re-layouts  3.75 us
  transfers between devices with their start and end apart: 12, of which 3 were waited for; matrix products, arithmetic and copies ran while one was open for 7% of the time, Pallas kernels for 22%

profile of v2, /device:TPU:15, one launch (start us, length us, event | category | flops | bytes accessed | tf_op | source)
XLA Modules:
  0.0 130.1 jit_solution(2435236015133365945)
XLA Ops:
  0.6 0.0 slice-start
  0.6 0.0 slice-start.2
  0.7 1.0 slice-done
  1.6 0.1 slice-done.2
  1.8 1.0 pad_maximum_fusion.1
  2.7 5.4 %collective-permute-start.3 = (bf16[1024,384]{1,0:T(8,128)(2,1)}, bf16[1024,384]{1,0:T(8,128)(2,1)S(1)}, u32[]{:S(2)}, u32[]{:S(2)}) collective-permute-start(bf16[1024,384]{1,0:T(8,128)(2,1)} %pad_maximum_fusion.1), channel_id=1, source_target_pairs={{4,8},{8,4},{12,16},{16,12},{20,24},{24,20},{28,32},{32,28},{36,40... | collective-permute-start | bytes 2359304 | tf_op jit(solution)/shard_map/ppermute | solution.py:30
  8.1 0.1 collective-permute-start.2
  8.3 0.9 tile.2
  9.2 8.0 %all-to-all-start = ((bf16[32,8,1536]{2,1,0:T(8,128)(2,1)}), bf16[32,8,1536]{2,1,0:T(8,128)(2,1)S(1)}, u32[]{:S(2)}, u32[]{:S(2)}) async-start(bf16[32,8,1536]{2,1,0:T(8,128)(2,1)} %tile.2), calls=%async_computation | async-start | bytes 1572864 | tf_op jit(solution)/shard_map/all_to_all | solution.py:287
  17.3 0.1 select_bitcast_fusion
  17.3 0.1 copy.17
  17.4 0.1 broadcast_in_dim.32
  17.5 0.6 copy.18
  18.1 0.1 broadcast_multiply_fusion.2
  18.3 0.2 broadcast_multiply_fusion.1
  18.5 1.9 %negate_select_fusion = (f32[512,128]{1,0:T(8,128)}, f32[512,128]{1,0:T(8,128)}) fusion(pred[128]{0:T(512)(128)(4,1)S(1)} %fusion.7, f32[512,56]{1,0:T(8,128)S(1)} %get-tuple-element.64, f32[512,56]{1,0:T(8,128)S(1)} %get-tuple-element.63, f32[512,16]{1,0:T(8,128)S(1)} %broadcast_multiply_fusion.2), kind=kLoop, calls=%fused_computation.2 | loop fusion | flops 262144 | bytes 786560 | tf_op jit(solution)/shard_map/jit(_where)/select_n | solution.py:63
  20.4 18.9 %all-to-all-done = bf16[32,8,1536]{2,1,0:T(8,128)(2,1)S(1)} async-done(((bf16[32,8,1536]{2,1,0:T(8,128)(2,1)}), bf16[32,8,1536]{2,1,0:T(8,128)(2,1)S(1)}, u32[]{:S(2)}, u32[]{:S(2)}) %all-to-all-start) | async-done | bytes 786464 | tf_op jit(solution)/shard_map/all_to_all | solution.py:287
  39.3 0.9 copy-done
  40.2 0.4 slice-done.1
  40.6 0.1 slice-done.3
  40.7 1.0 pad_maximum_fusion
  41.7 2.7 %collective-permute-start.1 = (bf16[1024,384]{1,0:T(8,128)(2,1)}, bf16[1024,384]{1,0:T(8,128)(2,1)}, u32[]{:S(2)}, u32[]{:S(2)}) collective-permute-start(bf16[1024,384]{1,0:T(8,128)(2,1)} %pad_maximum_fusion), channel_id=1, source_target_pairs={{4,8},{8,4},{12,16},{16,12},{20,24},{24,20},{28,32},{32,28},{36,40... | collective-permute-start | bytes 2359304 | tf_op jit(solution)/shard_map/ppermute | solution.py:30
  44.4 0.1 collective-permute-start
  44.5 0.0 collective-permute-done.3.refs_10_.refs_11_
  44.5 0.0 collective-permute-done.2.refs_8_.refs_9_
  44.5 0.9 copy-done.1
  45.4 0.2 copy-done.2
  45.6 12.9 %attend.2 = (bf16[512,768]{1,0:T(8,128)(2,1)}, f32[512,384]{1,0:T(8,128)}, f32[512,384]{1,0:T(8,128)}, bf16[1024,384]{1,0:T(8,128)(2,1)}, bf16[1024,384]{1,0:T(8,128)(2,1)}, /*index=5*/bf16[256,768]{1,0:T(8,128)(2,1)}) custom-call(s32[1]{0:T(128)} %bitcast.refs_0_, f32[12,512]{1,0:T(8,128)} %bitcast.22, f32[512,128]{1,0:T(8,128)} %get-tuple-element.56.refs_2_.refs_0_, ...), custom_call_target="tpu_custom_call" | custom-call | flops 2359296 | bytes 196608 | tf_op jit(solution)/shard_map/attend/pallas_call | solution.py:206
  58.5 1.5 %collective-permute-start.4 = (bf16[1024,384]{1,0:T(8,128)(2,1)}, bf16[1024,384]{1,0:T(8,128)(2,1)S(1)}, u32[]{:S(2)}, u32[]{:S(2)}) collective-permute-start(bf16[1024,384]{1,0:T(8,128)(2,1)} %get-tuple-element.37), channel_id=1, source_target_pairs={{0,4},{4,0},{8,12},{12,8},{16,20},{20,16},{24,28},{28,24},{32,36},... | collective-permute-start | bytes 2359304 | tf_op jit(solution)/shard_map/ppermute | solution.py:30
  60.0 6.2 %collective-permute-start.5 = (bf16[1024,384]{1,0:T(8,128)(2,1)}, bf16[1024,384]{1,0:T(8,128)(2,1)S(1)}, u32[]{:S(2)}, u32[]{:S(2)}) collective-permute-start(bf16[1024,384]{1,0:T(8,128)(2,1)} %get-tuple-element.38), channel_id=1, source_target_pairs={{4,8},{8,4},{12,16},{16,12},{20,24},{24,20},{28,32},{32,28},{36,40... | collective-permute-start | bytes 2359304 | tf_op jit(solution)/shard_map/ppermute | solution.py:30
  66.2 5.8 %all-to-all-start.1 = ((bf16[8,32,768]{2,1,0:T(8,128)(2,1)}), bf16[8,32,768]{2,1,0:T(8,128)(2,1)S(1)}, u32[]{:S(2)}, u32[]{:S(2)}) async-start(bf16[8,32,768]{2,1,0:T(8,128)(2,1)} %bitcast.20), calls=%async_computation.1 | async-start | bytes 786432 | tf_op jit(solution)/shard_map/all_to_all | solution.py:41
  72.1 0.0 collective-permute-done.1.refs_10_.refs_11_
  72.1 12.9 %attend.3 = (bf16[512,768]{1,0:T(8,128)(2,1)}, f32[512,384]{1,0:T(8,128)}, f32[512,384]{1,0:T(8,128)}, bf16[1024,384]{1,0:T(8,128)(2,1)}, bf16[1024,384]{1,0:T(8,128)(2,1)}, /*index=5*/bf16[256,768]{1,0:T(8,128)(2,1)}) custom-call(s32[1]{0:T(128)} %bitcast.refs_0_, f32[12,512]{1,0:T(8,128)} %bitcast.23, ...), custom_call_target="tpu_custom_call", output_to_operand_aliasing={{0}: (14, {})} | custom-call | flops 2359296 | bytes 196608 | tf_op jit(solution)/shard_map/attend/pallas_call | solution.py:206
  85.0 4.5 %all-to-all-done.1 = bf16[8,32,768]{2,1,0:T(8,128)(2,1)S(1)} async-done(((bf16[8,32,768]{2,1,0:T(8,128)(2,1)}), bf16[8,32,768]{2,1,0:T(8,128)(2,1)S(1)}, u32[]{:S(2)}, u32[]{:S(2)}) %all-to-all-start.1) | async-done | bytes 393248 | tf_op jit(solution)/shard_map/all_to_all | solution.py:41
  89.4 6.6 %all-to-all-start.2 = ((bf16[8,32,768]{2,1,0:T(8,128)(2,1)}), bf16[8,32,768]{2,1,0:T(8,128)(2,1)}, u32[]{:S(2)}, u32[]{:S(2)}) async-start(bf16[8,32,768]{2,1,0:T(8,128)(2,1)} %bitcast.21), calls=%async_computation.2 | async-start | bytes 786432 | tf_op jit(solution)/shard_map/all_to_all | solution.py:41
  96.1 0.6 collective-permute-start.6
  96.6 5.2 %collective-permute-start.7 = (bf16[1024,384]{1,0:T(8,128)(2,1)}, bf16[1024,384]{1,0:T(8,128)(2,1)S(1)}, u32[]{:S(2)}, u32[]{:S(2)}) collective-permute-start(bf16[1024,384]{1,0:T(8,128)(2,1)} %get-tuple-element.44), channel_id=1, source_target_pairs={{4,8},{8,4},{12,16},{16,12},{20,24},{24,20},{28,32},{32,28},{36,40... | collective-permute-start | bytes 2359304 | tf_op jit(solution)/shard_map/ppermute | solution.py:30
  101.8 0.7 reduce_sum.36
  102.5 0.0 all-to-all-done.2
  102.5 1.1 reduce_sum.37
  103.6 1.4 %maximum_bitcast_fusion = bf16[4,8,1536]{2,1,0:T(8,128)(2,1)} fusion(bf16[32,768]{1,0:T(8,128)(2,1)S(1)} %reduce_sum.37, bf16[32,768]{1,0:T(8,128)(2,1)} %reduce_sum.36), kind=kLoop, calls=%fused_computation.8 | loop fusion | flops 196608 | bytes 196608 | tf_op jit(solution)/shard_map/all_to_all | solution.py:41
  105.1 5.6 %all-to-all-start.3 = ((bf16[4,8,1536]{2,1,0:T(8,128)(2,1)}), bf16[4,8,1536]{2,1,0:T(8,128)(2,1)S(1)}, u32[]{:S(2)}, u32[]{:S(2)}) async-start(bf16[4,8,1536]{2,1,0:T(8,128)(2,1)} %maximum_bitcast_fusion), calls=%async_computation.3 | async-start | bytes 196608 | tf_op jit(solution)/shard_map/all_to_all | solution.py:41
  110.7 3.1 %finish.2 = (bf16[512,768]{1,0:T(8,128)(2,1)}, bf16[512,768]{1,0:T(8,128)(2,1)}) custom-call(f32[512,128]{1,0:T(8,128)} %get-tuple-element.56.refs_2_.refs_0_, f32[512,128]{1,0:T(8,128)} %get-tuple-element.55.refs_3_.refs_1_, f32[512,384]{1,0:T(8,128)} %get-tuple-element.45.refs_2_, f32[512,384]{1,0:T(8,128)} %get-tuple-element.46.refs_3_, ...), custom_call_target="tpu_custom_call" | custom-call | flops 1966080 | bytes 3932160 | tf_op jit(solution)/shard_map/finish/pallas_call | solution.py:257
  113.8 11.5 %all-to-all-done.3 = bf16[4,8,1536]{2,1,0:T(8,128)(2,1)S(1)} async-done(((bf16[4,8,1536]{2,1,0:T(8,128)(2,1)}), bf16[4,8,1536]{2,1,0:T(8,128)(2,1)S(1)}, u32[]{:S(2)}, u32[]{:S(2)}) %all-to-all-start.3) | async-done | bytes 98336 | tf_op jit(solution)/shard_map/all_to_all | solution.py:41
  125.3 0.6 pad_maximum_fusion.4
  126.0 0.9 copy-done.5
  126.8 0.3 copy-done.6
  127.1 3.0 %finish.3 = (bf16[512,768]{1,0:T(8,128)(2,1)}, bf16[512,768]{1,0:T(8,128)(2,1)}) custom-call(f32[512,128]{1,0:T(8,128)} %get-tuple-element.56.refs_2_.refs_0_, f32[512,128]{1,0:T(8,128)} %get-tuple-element.55.refs_3_.refs_1_, f32[512,384]{1,0:T(8,128)} %get-tuple-element.35.refs_2_, ...), custom_call_target="tpu_custom_call", output_to_operand_aliasing={{0}: (8, {}), {1}: (9, {})} | custom-call | flops 1966080 | bytes 3932160 | tf_op jit(solution)/shard_map/finish/pallas_call | solution.py:257
  (33 shorter events, 0.1 us)
Async XLA Ops:
  0.6 1.0 slice-start
  0.6 1.1 slice-start.2
  1.8 6.5 %copy-start.8 = (bf16[8,768]{1,0:T(8,128)(2,1)S(1)}, bf16[8,768]{1,0:T(8,128)(2,1)}, u32[]{:S(2)}) copy-start(bf16[8,768]{1,0:T(8,128)(2,1)} %param.13) | copy-start | bytes 36868
  1.8 6.5 %copy-start.9 = (bf16[8,768]{1,0:T(8,128)(2,1)S(1)}, bf16[8,768]{1,0:T(8,128)(2,1)}, u32[]{:S(2)}) copy-start(bf16[8,768]{1,0:T(8,128)(2,1)} %param.12) | copy-start | bytes 36868
  2.7 41.8 %collective-permute-start.3 = (bf16[1024,384]{1,0:T(8,128)(2,1)}, bf16[1024,384]{1,0:T(8,128)(2,1)S(1)}, u32[]{:S(2)}, u32[]{:S(2)}) collective-permute-start(bf16[1024,384]{1,0:T(8,128)(2,1)} %pad_maximum_fusion.1), channel_id=1, source_target_pairs={{4,8},{8,4},{12,16},{16,12},{20,24},{24,20},{28,32},{32,28},{36,40... | collective-permute-start | bytes 2359304 | tf_op jit(solution)/shard_map/ppermute | solution.py:30
  8.1 36.4 %collective-permute-start.2 = (bf16[1024,384]{1,0:T(8,128)(2,1)}, bf16[1024,384]{1,0:T(8,128)(2,1)S(1)}, u32[]{:S(2)}, u32[]{:S(2)}) collective-permute-start(bf16[1024,384]{1,0:T(8,128)(2,1)} %pad_maximum_fusion.1), channel_id=1, source_target_pairs={{0,4},{4,0},{8,12},{12,8},{16,20},{20,16},{24,28},{28,24},{32,36},... | collective-permute-start | bytes 2359304 | tf_op jit(solution)/shard_map/ppermute | solution.py:30
  9.2 8.0 %copy-start.10 = (s32[3,512]{1,0:T(4,128)S(1)}, s32[3,512]{1,0:T(4,128)}, u32[]{:S(2)}) copy-start(s32[3,512]{1,0:T(4,128)} %param.14) | copy-start | bytes 18436
  9.2 8.1 %copy-start.7 = (s32[128,128]{1,0:T(8,128)S(1)}, s32[128,128]{1,0:T(8,128)}, u32[]{:S(2)}) copy-start(s32[128,128]{1,0:T(8,128)} %param.15) | copy-start | bytes 196612
  9.2 30.1 %all-to-all-start = ((bf16[32,8,1536]{2,1,0:T(8,128)(2,1)}), bf16[32,8,1536]{2,1,0:T(8,128)(2,1)S(1)}, u32[]{:S(2)}, u32[]{:S(2)}) async-start(bf16[32,8,1536]{2,1,0:T(8,128)(2,1)} %tile.2), calls=%async_computation | async-start | bytes 1572864 | tf_op jit(solution)/shard_map/all_to_all | solution.py:287
  39.3 0.9 copy-start
  39.3 1.3 slice-start.1
  39.3 1.4 %slice-start.3 = ((bf16[512,768]{1,0:T(8,128)(2,1)}), bf16[512,384]{1,0:T(8,128)(2,1)S(1)}, s32[]{:S(2)}) async-start(bf16[512,768]{1,0:T(8,128)(2,1)} %refs_7_.3), calls=%async_computation.7 | async-start | bytes 786432 | tf_op jit(solution)/shard_map/slice | solution.py:283
  41.7 30.4 %collective-permute-start.1 = (bf16[1024,384]{1,0:T(8,128)(2,1)}, bf16[1024,384]{1,0:T(8,128)(2,1)}, u32[]{:S(2)}, u32[]{:S(2)}) collective-permute-start(bf16[1024,384]{1,0:T(8,128)(2,1)} %pad_maximum_fusion), channel_id=1, source_target_pairs={{4,8},{8,4},{12,16},{16,12},{20,24},{24,20},{28,32},{32,28},{36,40... | collective-permute-start | bytes 2359304 | tf_op jit(solution)/shard_map/ppermute | solution.py:30
  44.4 27.7 %collective-permute-start = (bf16[1024,384]{1,0:T(8,128)(2,1)}, bf16[1024,384]{1,0:T(8,128)(2,1)}, u32[]{:S(2)}, u32[]{:S(2)}) collective-permute-start(bf16[1024,384]{1,0:T(8,128)(2,1)} %pad_maximum_fusion), channel_id=1, source_target_pairs={{0,4},{4,0},{8,12},{12,8},{16,20},{20,16},{24,28},{28,24},{32,36},... | collective-permute-start | bytes 2359304 | tf_op jit(solution)/shard_map/ppermute | solution.py:30
  44.5 0.9 copy-start.1
  44.5 1.1 copy-start.2
  58.5 30.9 %collective-permute-start.4 = (bf16[1024,384]{1,0:T(8,128)(2,1)}, bf16[1024,384]{1,0:T(8,128)(2,1)S(1)}, u32[]{:S(2)}, u32[]{:S(2)}) collective-permute-start(bf16[1024,384]{1,0:T(8,128)(2,1)} %get-tuple-element.37), channel_id=1, source_target_pairs={{0,4},{4,0},{8,12},{12,8},{16,20},{20,16},{24,28},{28,24},{32,36},... | collective-permute-start | bytes 2359304 | tf_op jit(solution)/shard_map/ppermute | solution.py:30
  60.0 29.4 %collective-permute-start.5 = (bf16[1024,384]{1,0:T(8,128)(2,1)}, bf16[1024,384]{1,0:T(8,128)(2,1)S(1)}, u32[]{:S(2)}, u32[]{:S(2)}) collective-permute-start(bf16[1024,384]{1,0:T(8,128)(2,1)} %get-tuple-element.38), channel_id=1, source_target_pairs={{4,8},{8,4},{12,16},{16,12},{20,24},{24,20},{28,32},{32,28},{36,40... | collective-permute-start | bytes 2359304 | tf_op jit(solution)/shard_map/ppermute | solution.py:30
  66.2 23.2 %all-to-all-start.1 = ((bf16[8,32,768]{2,1,0:T(8,128)(2,1)}), bf16[8,32,768]{2,1,0:T(8,128)(2,1)S(1)}, u32[]{:S(2)}, u32[]{:S(2)}) async-start(bf16[8,32,768]{2,1,0:T(8,128)(2,1)} %bitcast.20), calls=%async_computation.1 | async-start | bytes 786432 | tf_op jit(solution)/shard_map/all_to_all | solution.py:41
  89.4 14.2 %copy-start.3 = (bf16[1024,384]{1,0:T(8,128)(2,1)}, bf16[1024,384]{1,0:T(8,128)(2,1)S(1)}, u32[]{:S(2)}) copy-start(bf16[1024,384]{1,0:T(8,128)(2,1)S(1)} %collective-permute-done.4.refs_4_.refs_5_) | copy-start | bytes 2359300
  89.4 14.2 %copy-start.4 = (bf16[1024,384]{1,0:T(8,128)(2,1)}, bf16[1024,384]{1,0:T(8,128)(2,1)S(1)}, u32[]{:S(2)}) copy-start(bf16[1024,384]{1,0:T(8,128)(2,1)S(1)} %collective-permute-done.5.refs_6_.refs_7_) | copy-start | bytes 2359300
  89.4 13.1 %all-to-all-start.2 = ((bf16[8,32,768]{2,1,0:T(8,128)(2,1)}), bf16[8,32,768]{2,1,0:T(8,128)(2,1)}, u32[]{:S(2)}, u32[]{:S(2)}) async-start(bf16[8,32,768]{2,1,0:T(8,128)(2,1)} %bitcast.21), calls=%async_computation.2 | async-start | bytes 786432 | tf_op jit(solution)/shard_map/all_to_all | solution.py:41
  96.1 29.9 %collective-permute-start.6 = (bf16[1024,384]{1,0:T(8,128)(2,1)}, bf16[1024,384]{1,0:T(8,128)(2,1)S(1)}, u32[]{:S(2)}, u32[]{:S(2)}) collective-permute-start(bf16[1024,384]{1,0:T(8,128)(2,1)} %get-tuple-element.43), channel_id=1, source_target_pairs={{0,4},{4,0},{8,12},{12,8},{16,20},{20,16},{24,28},{28,24},{32,36},... | collective-permute-start | bytes 2359304 | tf_op jit(solution)/shard_map/ppermute | solution.py:30
  96.6 29.3 %collective-permute-start.7 = (bf16[1024,384]{1,0:T(8,128)(2,1)}, bf16[1024,384]{1,0:T(8,128)(2,1)S(1)}, u32[]{:S(2)}, u32[]{:S(2)}) collective-permute-start(bf16[1024,384]{1,0:T(8,128)(2,1)} %get-tuple-element.44), channel_id=1, source_target_pairs={{4,8},{8,4},{12,16},{16,12},{20,24},{24,20},{28,32},{32,28},{36,40... | collective-permute-start | bytes 2359304 | tf_op jit(solution)/shard_map/ppermute | solution.py:30
  105.1 20.2 %all-to-all-start.3 = ((bf16[4,8,1536]{2,1,0:T(8,128)(2,1)}), bf16[4,8,1536]{2,1,0:T(8,128)(2,1)S(1)}, u32[]{:S(2)}, u32[]{:S(2)}) async-start(bf16[4,8,1536]{2,1,0:T(8,128)(2,1)} %maximum_bitcast_fusion), calls=%async_computation.3 | async-start | bytes 196608 | tf_op jit(solution)/shard_map/all_to_all | solution.py:41
  125.9 0.9 copy-start.5
  126.0 1.1 copy-start.6

commit v3 on v2

--- a/solution.py
+++ b/solution.py
@@ -77,17 +77,11 @@
     return combine(block.reshape(block.shape[0] // 8, 8, block.shape[1]), axis=0)
 
 
-def by_place(rows):
-    own, run = 8, 8
-    tiles = rows.reshape(-1, run, own, rows.shape[1])
-    return jnp.concatenate([tiles[r, place] for place in range(run) for r in range(tiles.shape[0])], axis=0)
-
-
-def attend_body(*refs, aliased):
+def attend_body(*refs, aliased, txt_own):
     (place_ref, bias_ref, cos_ref, sin_ref, q_ref, g_ref, ko_ref, vo_ref, ka_ref, va_ref, kb_ref, vb_ref, tk_ref,
      tv_ref) = refs[:14]
-    refs = refs[14 + (1 if aliased else 0):]
-    dq_ref, dko_ref, dvo_ref, da_ref, db_ref, dt_ref, s_scr, dp_scr, e_scr, kl_ref, vl_ref, kr_ref, vr_ref = refs
+    refs = refs[14 + (2 if aliased else 0):]
+    dq_ref, do_ref, da_ref, db_ref, dt_ref, s_scr, dp_scr, e_scr, kl_ref, vl_ref, kr_ref, vr_ref = refs
     even = place_ref[0] % 2 == 0
     for left_ref, right_ref, a_ref, b_ref in ((kl_ref, kr_ref, ka_ref, kb_ref), (vl_ref, vr_ref, va_ref, vb_ref)):
         left_ref[...] = jnp.where(even, b_ref[...], a_ref[...])
@@ -160,13 +154,12 @@
             part = slice(frame * f - cols.start, (frame + 1) * f - cols.start)
             dq_parts[frame] = dq_parts[frame] + dot(key, dscores[:, part], TN)
         if k_ref is ko_ref:
-            dko_ref[row:row + f, :] = key_term
-            dvo_ref[row:row + f, :] = value_term
+            do_ref[row:row + f, :] = key_term.astype(jnp.bfloat16)
+            do_ref[tok + row:tok + row + f, :] = value_term.astype(jnp.bfloat16)
         elif k_ref is tk_ref:
-            at = pl.multiple_of(pl.program_id(0) * D_HEAD, D_HEAD)
-            value_at = pl.multiple_of(at + dt_ref.shape[1] // 2, D_HEAD)
-            dt_ref[:, pl.ds(at, D_HEAD)] = by_place(key_term).astype(jnp.bfloat16)
-            dt_ref[:, pl.ds(value_at, D_HEAD)] = by_place(value_term).astype(jnp.bfloat16)
+            own = txt_own
+            pair = jnp.stack([term.reshape(-1, own, D_HEAD) for term in (key_term, value_term)], axis=1)
+            dt_ref[...] = pair.reshape(dt_ref.shape).astype(jnp.bfloat16)
         else:
             sides[k_ref is kr_ref, row] = key_term.astype(jnp.bfloat16), value_term.astype(jnp.bfloat16)
             if k_ref is kr_ref:
@@ -181,7 +174,7 @@
         dq_ref[cols, :] = unrotate(query_grad, cos_ref[cols, :], sin_ref[cols, :]).astype(jnp.bfloat16)
 
 
-def attend(place, bias, cosine, sine, query, grad, key, value, left, right, text, before, first, heads):
+def attend(txt_own, place, bias, cosine, sine, query, grad, key, value, left, right, text, before, first, heads):
     tok, width = query.shape
     txt = text.shape[0]
     all_heads = width // D_HEAD
@@ -198,23 +191,22 @@
     operands = [place, bias, cosine, sine, query, grad, key, value, left, left, right, right, text, text]
     aliases = {}
     if before is not None:
-        in_specs.append(pl.BlockSpec(memory_space=pl.ANY))
-        operands.append(before)
-        aliases = {len(operands) - 1: 0}
+        aliases = {len(operands): 0, len(operands) + 1: 4}
+        in_specs += [pl.BlockSpec(memory_space=pl.ANY)] * 2
+        operands += list(before)
     keys = 3 * tok + txt
     pairs = tok * (5 * FRAME + txt) * heads
     return pl.pallas_call(
-        functools.partial(attend_body, aliased=before is not None),
+        functools.partial(attend_body, aliased=before is not None, txt_own=txt_own),
         grid=(heads,),
         in_specs=in_specs,
-        out_specs=[here, upper, upper, both, both, whole((txt, 2 * wide))],
+        out_specs=[here, both, both, both, pl.BlockSpec((2 * txt, D_HEAD), lambda h: (0, first + h))],
         out_shape=[
             jax.ShapeDtypeStruct((tok, width), jnp.bfloat16),
-            jax.ShapeDtypeStruct((tok, wide), jnp.float32),
-            jax.ShapeDtypeStruct((tok, wide), jnp.float32),
             jax.ShapeDtypeStruct((2 * tok, wide), jnp.bfloat16),
             jax.ShapeDtypeStruct((2 * tok, wide), jnp.bfloat16),
-            jax.ShapeDtypeStruct((txt, 2 * wide), jnp.bfloat16),
+            jax.ShapeDtypeStruct((2 * tok, wide), jnp.bfloat16),
+            jax.ShapeDtypeStruct((2 * txt, width), jnp.bfloat16),
         ],
         scratch_shapes=[
             pltpu.VMEM((keys, tok), jnp.float32),
@@ -229,26 +221,26 @@
 
 
 def finish_body(*refs, aliased):
-    cos_ref, sin_ref, dk_ref, dv_ref, ak_ref, av_ref, bk_ref, bv_ref = refs[:8]
+    cos_ref, sin_ref, ok_ref, ov_ref, ak_ref, av_ref, bk_ref, bv_ref = refs[:8]
     key_ref, value_ref = refs[8 + (2 if aliased else 0):]
     up = lambda ref, cols: ref[:, cols].astype(jnp.float32)
     cosine, sine = cos_ref[...], sin_ref[...]
-    for head in range(dk_ref.shape[1] // D_HEAD):
+    for head in range(ok_ref.shape[1] // D_HEAD):
         cols = slice(head * D_HEAD, (head + 1) * D_HEAD)
-        key_grad = dk_ref[:, cols] + up(ak_ref, cols) + up(bk_ref, cols)
+        key_grad = up(ok_ref, cols) + up(ak_ref, cols) + up(bk_ref, cols)
         key_ref[:, cols] = unrotate(key_grad, cosine, sine).astype(jnp.bfloat16)
-        value_ref[:, cols] = (dv_ref[:, cols] + up(av_ref, cols) + up(bv_ref, cols)).astype(jnp.bfloat16)
-
-
-def finish(cosine, sine, key_own, value_own, back_a, back_b, before, first, width):
-    tok, wide = key_own.shape
+        value_ref[:, cols] = (up(ov_ref, cols) + up(av_ref, cols) + up(bv_ref, cols)).astype(jnp.bfloat16)
+
+
+def finish(cosine, sine, own, back_a, back_b, before, first, width):
+    tok, wide = own.shape[0] // 2, own.shape[1]
     step = tok // 2
     upper = pl.BlockSpec((step, wide), lambda r: (r, 0))
     lower = pl.BlockSpec((step, wide), lambda r: (tok // step + r, 0))
     table = pl.BlockSpec((step, D_HEAD), lambda r: (r, 0))
     here = pl.BlockSpec((step, wide), lambda r: (r, first * D_HEAD // wide))
-    in_specs = [table, table, upper, upper, upper, lower, upper, lower]
-    operands = [cosine, sine, key_own, value_own, back_a, back_a, back_b, back_b]
+    in_specs = [table, table] + [upper, lower] * 3
+    operands = [cosine, sine, own, own, back_a, back_a, back_b, back_b]
     aliases = {}
     if before is not None:
         in_specs += [pl.BlockSpec(memory_space=pl.ANY)] * 2
@@ -261,7 +253,7 @@
         out_specs=[here, here],
         out_shape=[jax.ShapeDtypeStruct((tok, width), jnp.bfloat16)] * 2,
         input_output_aliases=aliases,
-        compiler_params=pltpu.CompilerParams(vmem_limit_bytes=56 * 2**20),
+        compiler_params=pltpu.CompilerParams(vmem_limit_bytes=16 * 2**20),
         cost_estimate=pl.CostEstimate(flops=10 * tok * wide, bytes_accessed=20 * tok * wide, transcendentals=0),
         name="finish",
     )(*operands)
@@ -285,35 +277,33 @@
 
     halos = [halo(key_rot, value, 0)]
     text = lax.all_to_all(jnp.tile(text_own, (ctx_size, 1)), "ctx", 0, 0, tiled=True)
-    text, keys_later, values_later = lax.optimization_barrier((text, key_rot, value))
-    halos += [halo(keys_later, values_later, group) for group in range(1, len(sizes))]
     padded = jnp.pad(tile_mask, ((0, 0), (tiles, tiles)))
     block = lax.dynamic_slice(padded, (ctx_index * tiles, ctx_index * tiles), (tiles, 3 * tiles))
     bias = jnp.where(jnp.repeat(block.T > 0, TILE, axis=1), 0.0, BLOCKED).astype(jnp.float32)
-    cosine, sine = rope_tables(positions)
+    tables = rope_tables(positions)
+    halos[0], (cosine, sine), bias, keys_later, values_later = lax.optimization_barrier(
+        (halos[0], tables, bias, key_rot, value))
+    halos += [halo(keys_later, values_later, group) for group in range(1, len(sizes))]
     place = jnp.full((1,), ctx_index, jnp.int32)
-    query_grad, waiting, done, near_texts = None, None, None, []
+    before, waiting, done = None, None, None
     for group, (first, heads) in enumerate(zip(firsts, sizes)):
-        query_grad, key_own, value_own, to_even, to_odd, text_part = attend(
-            place, bias, cosine, sine, query_rot, grad_out, key_rot, value, *halos[group], text,
-            query_grad, first, heads)
+        query_grad, own, to_even, to_odd, text_part = attend(
+            text_key.shape[0], place, bias, cosine, sine, query_rot, grad_out, key_rot, value, *halos[group], text,
+            before, first, heads)
         if waiting is not None:
-            sent, ready = waiting[2:], (to_even, to_odd, text_part)
-            sent, (to_even, to_odd, text_part) = lax.optimization_barrier((sent, ready))
-            near_texts.append(sent[2])
-            done = finish(cosine, sine, *waiting[:2], *sent[:2], done, firsts[group - 1], width)
-        waiting = (key_own, value_own, exchange(to_even, "ctx", 0), exchange(to_odd, "ctx", 1), swap(text_part, near))
-    near_texts.append(waiting[4])
-    done = finish(cosine, sine, *waiting[:4], done, firsts[-1], width)
-    near_sums = jnp.concatenate([part_sum(part, len(near[0])) for part in near_texts], axis=1)
-    text_grads = part_sum(swap(near_sums, far), len(far[0]))
-    starts = [2 * first * D_HEAD for first in firsts]
-    text_key_grad, text_value_grad = (
-        jnp.concatenate([text_grads[:, at + k * heads * D_HEAD:at + (k + 1) * heads * D_HEAD]
-                         for at, heads in zip(starts, sizes)], axis=1)
-        for k in range(2)
-    )
-    return query_grad, done[0], done[1], text_key_grad, text_value_grad
+            done = finish(cosine, sine, *waiting, done, firsts[group - 1], width)
+        before = query_grad, text_part
+        waiting = (own, exchange(to_even, "ctx", 0), exchange(to_odd, "ctx", 1))
+    done = finish(cosine, sine, *waiting, done, firsts[-1], width)
+
+    def reduce_text(rows):
+        return part_sum(lax.all_to_all(rows, "ctx", 0, 0, tiled=True), ctx_size)
+
+    own = text_key.shape[0]
+    passes = jnp.minimum(tile_mask[0, 0] + 1, 1)
+    text_grads = lax.fori_loop(
+        0, passes, lambda step, _: reduce_text(lax.optimization_barrier((text_part, step))[0]), text_part[:2 * own])
+    return query_grad, done[0], done[1], text_grads[:own], text_grads[own:]
 
 
 def solution(mesh):

time: 131 us -> 119 us (0.908)
  the two profiles are of different devices: /device:TPU:15 before, /device:TPU:1 now
where the time goes in v3:
time: 119 us; the launch traced here: 118 us
  starting transfers between devices  39.9 us (34%)
  waiting for transfers between devices  33.2 us (28%)
  Pallas kernels  28 us (24%)
  local copies, waits for them, and re-layouts  9.36 us (8%)
  other arithmetic  6.16 us (5%)
  between operations  1.55 us (1%)
    pallas_call x2, Pallas kernels, attend(): pl.pallas_call(functools.partial(attend_body, aliased=before is not None,...  25.2 us
    all_to_all x1, waiting for transfers between devices, reduce_text(): return part_sum(lax.all_to_all(rows, 'ctx', 0, 0, tiled=True), ctx_size)  21.8 us
    ppermute x8, starting transfers between devices, exchange(): return lax.ppermute(block, axis, route)  14.8 us
    all_to_all x1, starting transfers between devices, reduce_text(): return part_sum(lax.all_to_all(rows, 'ctx', 0, 0, tiled=True), ctx_size)  13.5 us
    all_to_all x1, starting transfers between devices, shards(): lax.all_to_all(jnp.tile(text_own, (ctx_size, 1)), 'ctx', 0, 0, tiled=True)  11.6 us
    all_to_all x1, waiting for transfers between devices, shards(): lax.all_to_all(jnp.tile(text_own, (ctx_size, 1)), 'ctx', 0, 0, tiled=True)  10.9 us
    unnamed x30, local copies, waits for them, and re-layouts  3.81 us
    pallas_call x2, Pallas kernels, finish(): pl.pallas_call(functools.partial(finish_body, aliased=before is not None)...  2.83 us
  transfers between devices with their start and end apart: 10, of which 3 were waited for; matrix products, arithmetic and copies ran while one was open for 8% of the time, Pallas kernels for 23%

profile of v3, /device:TPU:1, one launch (start us, length us, event | category | flops | bytes accessed | tf_op | source)
XLA Modules:
  0.0 118.2 jit_solution(9045918493979221145)
XLA Ops:
  0.6 0.0 slice-start
  0.6 0.0 slice-start.2
  0.7 1.0 slice-done
  1.6 0.1 slice-done.2
  1.8 1.0 pad_maximum_fusion
  2.7 2.0 %collective-permute-start = (bf16[1024,384]{1,0:T(8,128)(2,1)}, bf16[1024,384]{1,0:T(8,128)(2,1)S(1)}, u32[]{:S(2)}, u32[]{:S(2)}) collective-permute-start(bf16[1024,384]{1,0:T(8,128)(2,1)} %pad_maximum_fusion), channel_id=1, source_target_pairs={{0,4},{4,0},{8,12},{12,8},{16,20},{20,16},{24,28},{28,24},{32,36},... | collective-permute-start | bytes 2359304 | tf_op jit(solution)/shard_map/ppermute | solution.py:30
  4.8 0.7 collective-permute-start.1
  5.5 0.1 broadcast_multiply_fusion.2
  5.7 0.2 broadcast_multiply_fusion.1
  5.9 1.9 %negate_select_fusion = (f32[512,128]{1,0:T(8,128)}, f32[512,128]{1,0:T(8,128)}) fusion(pred[128]{0:T(512)(128)(4,1)S(1)} %fusion.7, f32[512,56]{1,0:T(8,128)S(1)} %get-tuple-element.116, f32[512,56]{1,0:T(8,128)S(1)} %get-tuple-element.115, f32[512,16]{1,0:T(8,128)S(1)} %broadcast_multiply_fusion.2), kind=kLoop, calls=%fused_computation.2 | loop fusion | flops 262144 | bytes 786560 | tf_op jit(solution)/shard_map/jit(_where)/select_n | solution.py:63
  7.9 0.9 tile.2
  8.8 11.6 %all-to-all-start.1 = ((bf16[32,8,1536]{2,1,0:T(8,128)(2,1)}), bf16[32,8,1536]{2,1,0:T(8,128)(2,1)S(1)}, u32[]{:S(2)}, u32[]{:S(2)}) async-start(bf16[32,8,1536]{2,1,0:T(8,128)(2,1)} %tile.2), calls=%async_computation.1 | async-start | bytes 1572864 | tf_op jit(solution)/shard_map/all_to_all | solution.py:279
  20.4 0.1 select_bitcast_fusion
  20.5 0.1 copy.17
  20.6 0.1 broadcast_in_dim.33
  20.7 0.6 copy.18
  21.3 0.4 collective-permute-done.refs_8_.refs_9_
  21.7 0.0 collective-permute-done.1.refs_10_.refs_11_
  21.7 0.9 copy-done.7
  22.7 0.2 copy-done.6
  22.9 0.8 slice-done.1
  23.6 0.1 slice-done.3
  23.8 1.0 pad_maximum_fusion.1
  24.7 4.4 %collective-permute-start.2 = (bf16[1024,384]{1,0:T(8,128)(2,1)}, bf16[1024,384]{1,0:T(8,128)(2,1)S(1)}, u32[]{:S(2)}, u32[]{:S(2)}) collective-permute-start(bf16[1024,384]{1,0:T(8,128)(2,1)} %pad_maximum_fusion.1), channel_id=1, source_target_pairs={{0,4},{4,0},{8,12},{12,8},{16,20},{20,16},{24,28},{28,24},{32,36},... | collective-permute-start | bytes 2359304 | tf_op jit(solution)/shard_map/ppermute | solution.py:30
  29.2 0.7 collective-permute-start.3
  29.9 10.9 %all-to-all-done.1 = bf16[32,8,1536]{2,1,0:T(8,128)(2,1)S(1)} async-done(((bf16[32,8,1536]{2,1,0:T(8,128)(2,1)}), bf16[32,8,1536]{2,1,0:T(8,128)(2,1)S(1)}, u32[]{:S(2)}, u32[]{:S(2)}) %all-to-all-start.1) | async-done | bytes 786464 | tf_op jit(solution)/shard_map/all_to_all | solution.py:279
  40.8 0.9 copy-done.5
  41.7 12.5 %attend.2 = (bf16[512,768]{1,0:T(8,128)(2,1)}, bf16[1024,384]{1,0:T(8,128)(2,1)}, bf16[1024,384]{1,0:T(8,128)(2,1)}, bf16[1024,384]{1,0:T(8,128)(2,1)}, bf16[512,768]{1,0:T(8,128)(2,1)S(1)}) custom-call(s32[1]{0:T(128)} %bitcast.1.refs_0_, f32[12,512]{1,0:T(8,128)} %bitcast.19, f32[512,128]{1,0:T(8,128)} %get-tuple-element.80.refs_2_.refs_0_, ...), custom_call_target="tpu_custom_call" | custom-call | flops 2359296 | bytes 196608 | tf_op jit(solution)/shard_map/attend/pallas_call | solution.py:199
  54.3 0.1 collective-permute-start.6
  54.3 0.7 collective-permute-start.7
  55.1 0.0 collective-permute-done.2.refs_8_.refs_9_
  55.1 0.0 copy-start.8
  55.1 0.0 collective-permute-done.3.refs_10_.refs_11_
  55.1 0.0 copy-start.9
  55.1 0.8 copy-done.8
  56.0 0.3 copy-done.9
  56.2 12.7 %attend.3 = (bf16[512,768]{1,0:T(8,128)(2,1)}, bf16[1024,384]{1,0:T(8,128)(2,1)}, bf16[1024,384]{1,0:T(8,128)(2,1)}, bf16[1024,384]{1,0:T(8,128)(2,1)}, bf16[512,768]{1,0:T(8,128)(2,1)S(1)}) custom-call(s32[1]{0:T(128)} %bitcast.1.refs_0_, f32[12,512]{1,0:T(8,128)} %bitcast.20, ...), custom_call_target="tpu_custom_call", output_to_operand_aliasing={{0}: (14, {}), {4}: (15, {})} | custom-call | flops 2359296 | bytes 196608 | tf_op jit(solution)/shard_map/attend/pallas_call | solution.py:199
  68.9 5.5 %collective-permute-start.4 = (bf16[1024,384]{1,0:T(8,128)(2,1)}, bf16[1024,384]{1,0:T(8,128)(2,1)S(1)}, u32[]{:S(2)}, u32[]{:S(2)}) collective-permute-start(bf16[1024,384]{1,0:T(8,128)(2,1)} %get-tuple-element.90), channel_id=1, source_target_pairs={{0,4},{4,0},{8,12},{12,8},{16,20},{20,16},{24,28},{28,24},{32,36},... | collective-permute-start | bytes 2359304 | tf_op jit(solution)/shard_map/ppermute | solution.py:30
  74.4 0.7 collective-permute-start.5
  75.1 0.5 slice.41
  76.3 0.6 slice.40
  76.9 1.4 %finish.2 = (bf16[512,768]{1,0:T(8,128)(2,1)}, bf16[512,768]{1,0:T(8,128)(2,1)}) custom-call(f32[512,128]{1,0:T(8,128)S(1)} %copy-done.1, f32[512,128]{1,0:T(8,128)S(1)} %copy-done, bf16[1024,384]{1,0:T(8,128)(2,1)S(1)} %copy-done.2, bf16[1024,384]{1,0:T(8,128)(2,1)S(1)} %copy-done.2, bf16[1024,384]{1,0:T(8,128)(2,1)S(1)} %collective-permute-done.6.refs_4_.refs_5_, ...), custom_call_target="tpu_custom_call" | custom-call | flops 1966080 | bytes 3932160 | tf_op jit(solution)/shard_map/finish/pallas_call | solution.py:249
  78.3 37.1 %while.12 = (s32[]{:T(128)}, bf16[16,768]{1,0:T(8,128)(2,1)}, s32[]{:T(128)}, bf16[512,768]{1,0:T(8,128)(2,1)}, s32[]{:T(128)}, /*index=5*/bf16[]{:T(256)}) while((s32[]{:T(128)}, bf16[16,768]{1,0:T(8,128)(2,1)}, s32[]{:T(128)}, bf16[512,768]{1,0:T(8,128)(2,1)}, s32[]{:T(128)}, /*index=5*/bf16[]{:T(256)}) %tuple.42), condition=%wide.region_2.3_spmd, body=%wide.region_0.2_spmd.sunk | while | flops 380930 | bytes 3170407 | solution.py:304
  78.3 13.5 %all-to-all-start = ((bf16[32,16,768]{2,1,0:T(8,128)(2,1)}), bf16[32,16,768]{2,1,0:T(8,128)(2,1)}, u32[]{:S(2)}, u32[]{:S(2)}) async-start(bf16[32,16,768]{2,1,0:T(8,128)(2,1)} %bitcast.14), calls=%async_computation | async-start | bytes 1572864 | tf_op jit(solution)/shard_map/while/body/all_to_all | solution.py:300
  91.8 21.8 %all-to-all-done = bf16[32,16,768]{2,1,0:T(8,128)(2,1)} async-done(((bf16[32,16,768]{2,1,0:T(8,128)(2,1)}), bf16[32,16,768]{2,1,0:T(8,128)(2,1)}, u32[]{:S(2)}, u32[]{:S(2)}) %all-to-all-start) | async-done | bytes 786464 | tf_op jit(solution)/shard_map/while/body/all_to_all | solution.py:300
  113.6 1.9 %reduce_sum.13 = bf16[16,768]{1,0:T(8,128)(2,1)} reduce(bf16[32,16,768]{2,1,0:T(8,128)(2,1)} %all-to-all-done, bf16[]{:T(256)} %constant.74.clone.1..sunk), dimensions={0}, to_apply=%region_1.1 | reduce | flops 380928 | bytes 811010 | tf_op jit(solution)/shard_map/while/body/reduce_sum | solution.py:46
  115.5 1.3 %fusion.9 = (bf16[8,768]{1,0:T(8,128)(2,1)}, bf16[8,768]{1,0:T(8,128)(2,1)}) fusion(bf16[16,768]{1,0:T(8,128)(2,1)} %get-tuple-element.100), kind=kLoop, calls=%fused_computation.31 | loop fusion | bytes 49152 | tf_op jit(solution)/shard_map/slice | solution.py:306
  116.8 1.4 %finish.3 = (bf16[512,768]{1,0:T(8,128)(2,1)}, bf16[512,768]{1,0:T(8,128)(2,1)}) custom-call(f32[512,128]{1,0:T(8,128)S(1)} %copy-done.1, f32[512,128]{1,0:T(8,128)S(1)} %copy-done, bf16[1024,384]{1,0:T(8,128)(2,1)S(1)} %copy-done.3, bf16[1024,384]{1,0:T(8,128)(2,1)S(1)} %copy-done.3, ...), custom_call_target="tpu_custom_call", output_to_operand_aliasing={{0}: (8, {}), {1}: (9, {})} | custom-call | flops 1966080 | bytes 3932160 | tf_op jit(solution)/shard_map/finish/pallas_call | solution.py:249
  (34 shorter events, 0.1 us)
Async XLA Ops:
  0.6 1.0 slice-start
  0.6 1.1 slice-start.2
  1.8 3.8 %copy-start.13 = (s32[3,512]{1,0:T(4,128)S(1)}, s32[3,512]{1,0:T(4,128)}, u32[]{:S(2)}) copy-start(s32[3,512]{1,0:T(4,128)} %param.16) | copy-start | bytes 18436
  1.8 3.9 %copy-start.11 = (bf16[8,768]{1,0:T(8,128)(2,1)S(1)}, bf16[8,768]{1,0:T(8,128)(2,1)}, u32[]{:S(2)}) copy-start(bf16[8,768]{1,0:T(8,128)(2,1)} %param.15) | copy-start | bytes 36868
  1.8 3.9 %copy-start.12 = (bf16[8,768]{1,0:T(8,128)(2,1)S(1)}, bf16[8,768]{1,0:T(8,128)(2,1)}, u32[]{:S(2)}) copy-start(bf16[8,768]{1,0:T(8,128)(2,1)} %param.14) | copy-start | bytes 36868
  2.7 19.0 %collective-permute-start = (bf16[1024,384]{1,0:T(8,128)(2,1)}, bf16[1024,384]{1,0:T(8,128)(2,1)S(1)}, u32[]{:S(2)}, u32[]{:S(2)}) collective-permute-start(bf16[1024,384]{1,0:T(8,128)(2,1)} %pad_maximum_fusion), channel_id=1, source_target_pairs={{0,4},{4,0},{8,12},{12,8},{16,20},{20,16},{24,28},{28,24},{32,36},... | collective-permute-start | bytes 2359304 | tf_op jit(solution)/shard_map/ppermute | solution.py:30
  4.8 17.0 %collective-permute-start.1 = (bf16[1024,384]{1,0:T(8,128)(2,1)}, bf16[1024,384]{1,0:T(8,128)(2,1)S(1)}, u32[]{:S(2)}, u32[]{:S(2)}) collective-permute-start(bf16[1024,384]{1,0:T(8,128)(2,1)} %pad_maximum_fusion), channel_id=1, source_target_pairs={{4,8},{8,4},{12,16},{16,12},{20,24},{24,20},{28,32},{32,28},{36,40... | collective-permute-start | bytes 2359304 | tf_op jit(solution)/shard_map/ppermute | solution.py:30
  8.8 11.6 %copy-start.10 = (s32[128,128]{1,0:T(8,128)S(1)}, s32[128,128]{1,0:T(8,128)}, u32[]{:S(2)}) copy-start(s32[128,128]{1,0:T(8,128)} %param.17) | copy-start | bytes 196612
  8.8 32.0 %all-to-all-start.1 = ((bf16[32,8,1536]{2,1,0:T(8,128)(2,1)}), bf16[32,8,1536]{2,1,0:T(8,128)(2,1)S(1)}, u32[]{:S(2)}, u32[]{:S(2)}) async-start(bf16[32,8,1536]{2,1,0:T(8,128)(2,1)} %tile.2), calls=%async_computation.1 | async-start | bytes 1572864 | tf_op jit(solution)/shard_map/all_to_all | solution.py:279
  21.7 1.2 copy-start.6
  21.7 0.9 copy-start.7
  22.7 1.0 slice-start.1
  22.7 1.1 slice-start.3
  24.7 30.3 %collective-permute-start.2 = (bf16[1024,384]{1,0:T(8,128)(2,1)}, bf16[1024,384]{1,0:T(8,128)(2,1)S(1)}, u32[]{:S(2)}, u32[]{:S(2)}) collective-permute-start(bf16[1024,384]{1,0:T(8,128)(2,1)} %pad_maximum_fusion.1), channel_id=1, source_target_pairs={{0,4},{4,0},{8,12},{12,8},{16,20},{20,16},{24,28},{28,24},{32,36},... | collective-permute-start | bytes 2359304 | tf_op jit(solution)/shard_map/ppermute | solution.py:30
  29.2 25.9 %collective-permute-start.3 = (bf16[1024,384]{1,0:T(8,128)(2,1)}, bf16[1024,384]{1,0:T(8,128)(2,1)S(1)}, u32[]{:S(2)}, u32[]{:S(2)}) collective-permute-start(bf16[1024,384]{1,0:T(8,128)(2,1)} %pad_maximum_fusion.1), channel_id=1, source_target_pairs={{4,8},{8,4},{12,16},{16,12},{20,24},{24,20},{28,32},{32,28},{36,40... | collective-permute-start | bytes 2359304 | tf_op jit(solution)/shard_map/ppermute | solution.py:30
  40.8 0.9 copy-start.5
  54.3 22.6 %collective-permute-start.6 = (bf16[1024,384]{1,0:T(8,128)(2,1)}, bf16[1024,384]{1,0:T(8,128)(2,1)S(1)}, u32[]{:S(2)}, u32[]{:S(2)}) collective-permute-start(bf16[1024,384]{1,0:T(8,128)(2,1)} %get-tuple-element.93), channel_id=1, source_target_pairs={{0,4},{4,0},{8,12},{12,8},{16,20},{20,16},{24,28},{28,24},{32,36},... | collective-permute-start | bytes 2359304 | tf_op jit(solution)/shard_map/ppermute | solution.py:30
  54.3 22.5 %collective-permute-start.7 = (bf16[1024,384]{1,0:T(8,128)(2,1)}, bf16[1024,384]{1,0:T(8,128)(2,1)S(1)}, u32[]{:S(2)}, u32[]{:S(2)}) collective-permute-start(bf16[1024,384]{1,0:T(8,128)(2,1)} %get-tuple-element.94), channel_id=1, source_target_pairs={{4,8},{8,4},{12,16},{16,12},{20,24},{24,20},{28,32},{32,28},{36,40... | collective-permute-start | bytes 2359304 | tf_op jit(solution)/shard_map/ppermute | solution.py:30
  55.1 0.9 copy-start.8
  55.1 1.1 copy-start.9
  56.2 20.7 %copy-start = (f32[512,128]{1,0:T(8,128)S(1)}, f32[512,128]{1,0:T(8,128)}, u32[]{:S(2)}) copy-start(f32[512,128]{1,0:T(8,128)} %get-tuple-element.81.refs_3_.refs_1_) | copy-start | bytes 786436
  56.2 20.7 %copy-start.1 = (f32[512,128]{1,0:T(8,128)S(1)}, f32[512,128]{1,0:T(8,128)}, u32[]{:S(2)}) copy-start(f32[512,128]{1,0:T(8,128)} %get-tuple-element.80.refs_2_.refs_0_) | copy-start | bytes 786436
  56.2 20.7 %copy-start.2 = (bf16[1024,384]{1,0:T(8,128)(2,1)S(1)}, bf16[1024,384]{1,0:T(8,128)(2,1)}, u32[]{:S(2)}) copy-start(bf16[1024,384]{1,0:T(8,128)(2,1)} %get-tuple-element.92.refs_2_.refs_3_) | copy-start | bytes 2359300
  68.9 9.4 %copy-start.4 = (bf16[512,768]{1,0:T(8,128)(2,1)}, bf16[512,768]{1,0:T(8,128)(2,1)S(1)}, u32[]{:S(2)}) copy-start(bf16[512,768]{1,0:T(8,128)(2,1)S(1)} %get-tuple-element.146) | copy-start | bytes 2359300
  68.9 47.9 %collective-permute-start.4 = (bf16[1024,384]{1,0:T(8,128)(2,1)}, bf16[1024,384]{1,0:T(8,128)(2,1)S(1)}, u32[]{:S(2)}, u32[]{:S(2)}) collective-permute-start(bf16[1024,384]{1,0:T(8,128)(2,1)} %get-tuple-element.90), channel_id=1, source_target_pairs={{0,4},{4,0},{8,12},{12,8},{16,20},{20,16},{24,28},{28,24},{32,36},... | collective-permute-start | bytes 2359304 | tf_op jit(solution)/shard_map/ppermute | solution.py:30
  74.4 42.4 %collective-permute-start.5 = (bf16[1024,384]{1,0:T(8,128)(2,1)}, bf16[1024,384]{1,0:T(8,128)(2,1)S(1)}, u32[]{:S(2)}, u32[]{:S(2)}) collective-permute-start(bf16[1024,384]{1,0:T(8,128)(2,1)} %get-tuple-element.91), channel_id=1, source_target_pairs={{4,8},{8,4},{12,16},{16,12},{20,24},{24,20},{28,32},{32,28},{36,40... | collective-permute-start | bytes 2359304 | tf_op jit(solution)/shard_map/ppermute | solution.py:30
  78.3 38.5 %copy-start.3 = (bf16[1024,384]{1,0:T(8,128)(2,1)S(1)}, bf16[1024,384]{1,0:T(8,128)(2,1)}, u32[]{:S(2)}) copy-start(bf16[1024,384]{1,0:T(8,128)(2,1)} %get-tuple-element.89.refs_2_.refs_3_) | copy-start | bytes 2359300
  78.3 35.3 %all-to-all-start = ((bf16[32,16,768]{2,1,0:T(8,128)(2,1)}), bf16[32,16,768]{2,1,0:T(8,128)(2,1)}, u32[]{:S(2)}, u32[]{:S(2)}) async-start(bf16[32,16,768]{2,1,0:T(8,128)(2,1)} %bitcast.14), calls=%async_computation | async-start | bytes 1572864 | tf_op jit(solution)/shard_map/while/body/all_to_all | solution.py:300

commit v4 on v3

--- a/solution.py
+++ b/solution.py
@@ -214,7 +214,7 @@
             pltpu.VMEM((keys, tok), jnp.bfloat16),
         ] + [pltpu.VMEM((tok, D_HEAD), jnp.bfloat16)] * 4,
         input_output_aliases=aliases,
-        compiler_params=pltpu.CompilerParams(vmem_limit_bytes=56 * 2**20),
+        compiler_params=pltpu.CompilerParams(vmem_limit_bytes=60 * 2**20),
         cost_estimate=pl.CostEstimate(flops=pairs, bytes_accessed=tok * wide, transcendentals=0),
         name="attend",
     )(*operands)
@@ -270,20 +270,22 @@
     text_own = jnp.concatenate([text_key, text_value], axis=1)
     near, far = text_groups(ctx_size)
 
-    def halo(keys, values, group):
+    def packed(keys, values, group):
         cols = slice(firsts[group] * D_HEAD, (firsts[group] + sizes[group]) * D_HEAD)
-        pair = jnp.concatenate([keys[:, cols], values[:, cols]], axis=0)
-        return exchange(pair, "ctx", 0), exchange(pair, "ctx", 1)
-
-    halos = [halo(key_rot, value, 0)]
+        return jnp.concatenate([keys[:, cols], values[:, cols]], axis=0)
+
+    pair = packed(key_rot, value, 0)
+    halos = [(exchange(pair, "ctx", 0), exchange(pair, "ctx", 1))]
     text = lax.all_to_all(jnp.tile(text_own, (ctx_size, 1)), "ctx", 0, 0, tiled=True)
     padded = jnp.pad(tile_mask, ((0, 0), (tiles, tiles)))
     block = lax.dynamic_slice(padded, (ctx_index * tiles, ctx_index * tiles), (tiles, 3 * tiles))
     bias = jnp.where(jnp.repeat(block.T > 0, TILE, axis=1), 0.0, BLOCKED).astype(jnp.float32)
     tables = rope_tables(positions)
-    halos[0], (cosine, sine), bias, keys_later, values_later = lax.optimization_barrier(
-        (halos[0], tables, bias, key_rot, value))
-    halos += [halo(keys_later, values_later, group) for group in range(1, len(sizes))]
+    near_pair, keys_later, values_later = lax.optimization_barrier((halos[0][0], key_rot, value))
+    pairs = [packed(keys_later, values_later, group) for group in range(1, len(sizes))]
+    first_halves = [exchange(pair, "ctx", 0) for pair in pairs]
+    far_pair, (cosine, sine), bias, pairs = lax.optimization_barrier((halos[0][1], tables, bias, pairs))
+    halos = [(near_pair, far_pair)] + [(half, exchange(pair, "ctx", 1)) for half, pair in zip(first_halves, pairs)]
     place = jnp.full((1,), ctx_index, jnp.int32)
     before, waiting, done = None, None, None
     for group, (first, heads) in enumerate(zip(firsts, sizes)):
@@ -302,7 +304,7 @@
     own = text_key.shape[0]
     passes = jnp.minimum(tile_mask[0, 0] + 1, 1)
     text_grads = lax.fori_loop(
-        0, passes, lambda step, _: reduce_text(lax.optimization_barrier((text_part, step))[0]), text_part[:2 * own])
+        0, passes, lambda step, _: reduce_text(lax.optimization_barrier((text_part, step))[0]), jnp.concatenate([text_key, text_value], axis=0))
     return query_grad, done[0], done[1], text_grads[:own], text_grads[own:]
 
 

time: 119 us -> 116 us (0.975)
  the two profiles are of different devices: /device:TPU:1 before, /device:TPU:15 now
where the time goes in v4:
time: 116 us; the launch traced here: 114 us
  starting transfers between devices  40.8 us (35%)
  Pallas kernels  29.3 us (25%)
  waiting for transfers between devices  29 us (25%)
  local copies, waits for them, and re-layouts  8.02 us (7%)
  other arithmetic  5.59 us (5%)
  between operations  1.55 us (1%)
    pallas_call x2, Pallas kernels, attend(): pl.pallas_call(functools.partial(attend_body, aliased=before is not None,...  25.2 us
    ppermute x8, starting transfers between devices, exchange(): return lax.ppermute(block, axis, route)  24.4 us
    all_to_all x1, waiting for transfers between devices, reduce_text(): return part_sum(lax.all_to_all(rows, 'ctx', 0, 0, tiled=True), ctx_size)  20.1 us
    all_to_all x1, starting transfers between devices, reduce_text(): return part_sum(lax.all_to_all(rows, 'ctx', 0, 0, tiled=True), ctx_size)  9.65 us
    ppermute x8, waiting for transfers between devices, exchange(): return lax.ppermute(block, axis, route)  8.01 us
    all_to_all x1, starting transfers between devices, shards(): lax.all_to_all(jnp.tile(text_own, (ctx_size, 1)), 'ctx', 0, 0, tiled=True)  6.76 us
    pallas_call x2, Pallas kernels, finish(): pl.pallas_call(functools.partial(finish_body, aliased=before is not None)...  4.07 us
    unnamed x28, local copies, waits for them, and re-layouts  3.28 us
  transfers between devices with their start and end apart: 10, of which 4 were waited for; matrix products, arithmetic and copies ran while one was open for 8% of the time, Pallas kernels for 23%

profile of v4, /device:TPU:15, one launch (start us, length us, event | category | flops | bytes accessed | tf_op | source)
XLA Modules:
  0.0 114.3 jit_solution(8209526952347803845)
XLA Ops:
  0.6 0.0 slice-start
  0.6 0.0 slice-start.2
  0.7 1.0 slice-done
  1.6 0.1 slice-done.2
  1.8 1.0 pad_maximum_fusion
  2.7 0.5 collective-permute-start.1
  3.3 6.1 %collective-permute-start = (bf16[1024,384]{1,0:T(8,128)(2,1)}, bf16[1024,384]{1,0:T(8,128)(2,1)S(1)}, u32[]{:S(2)}, u32[]{:S(2)}) collective-permute-start(bf16[1024,384]{1,0:T(8,128)(2,1)} %pad_maximum_fusion), channel_id=1, source_target_pairs={{4,8},{8,4},{12,16},{16,12},{20,24},{24,20},{28,32},{32,28},{36,40... | collective-permute-start | bytes 2359304 | tf_op jit(solution)/shard_map/ppermute | solution.py:30
  9.3 0.0 copy-done.12
  9.4 0.1 broadcast_multiply_fusion.2
  9.6 0.2 broadcast_multiply_fusion.1
  9.8 1.9 %negate_select_fusion = (f32[512,128]{1,0:T(8,128)}, f32[512,128]{1,0:T(8,128)}) fusion(pred[128]{0:T(512)(128)(4,1)S(1)} %fusion.7, f32[512,56]{1,0:T(8,128)S(1)} %get-tuple-element.118, f32[512,56]{1,0:T(8,128)S(1)} %get-tuple-element.117, f32[512,16]{1,0:T(8,128)S(1)} %broadcast_multiply_fusion.2), kind=kLoop, calls=%fused_computation.2 | loop fusion | flops 262144 | bytes 786560 | tf_op jit(solution)/shard_map/jit(_where)/select_n | solution.py:63
  11.7 0.9 tile.2
  12.6 6.8 %all-to-all-start.1 = ((bf16[32,8,1536]{2,1,0:T(8,128)(2,1)}), bf16[32,8,1536]{2,1,0:T(8,128)(2,1)S(1)}, u32[]{:S(2)}, u32[]{:S(2)}) async-start(bf16[32,8,1536]{2,1,0:T(8,128)(2,1)} %tile.2), calls=%async_computation.1 | async-start | bytes 1572864 | tf_op jit(solution)/shard_map/all_to_all | solution.py:279
  19.4 0.1 select_bitcast_fusion
  19.5 0.1 copy.17
  19.6 0.1 broadcast_in_dim.33
  19.7 0.6 copy.18
  20.3 1.0 collective-permute-done.1.refs_8_.refs_9_
  21.3 0.9 copy-done.5
  22.2 1.0 pad_maximum_fusion.1
  23.2 7.0 %collective-permute-done.refs_10_.refs_11_ = bf16[1024,384]{1,0:T(8,128)(2,1)S(1)} collective-permute-done((bf16[1024,384]{1,0:T(8,128)(2,1)}, bf16[1024,384]{1,0:T(8,128)(2,1)S(1)}, u32[]{:S(2)}, u32[]{:S(2)}) %collective-permute-start) | collective-permute-done | bytes 786464 | tf_op jit(solution)/shard_map/ppermute | solution.py:30
  30.1 8.1 %collective-permute-start.3 = (bf16[1024,384]{1,0:T(8,128)(2,1)}, bf16[1024,384]{1,0:T(8,128)(2,1)S(1)}, u32[]{:S(2)}, u32[]{:S(2)}) collective-permute-start(bf16[1024,384]{1,0:T(8,128)(2,1)} %pad_maximum_fusion.1), channel_id=1, source_target_pairs={{4,8},{8,4},{12,16},{16,12},{20,24},{24,20},{28,32},{32,28},{36,40... | collective-permute-start | bytes 2359304 | tf_op jit(solution)/shard_map/ppermute | solution.py:30
  38.2 0.1 collective-permute-start.2
  38.3 0.9 all-to-all-done.1
  39.2 0.9 copy-done.4
  40.1 12.6 %attend.2 = (bf16[512,768]{1,0:T(8,128)(2,1)}, bf16[1024,384]{1,0:T(8,128)(2,1)}, bf16[1024,384]{1,0:T(8,128)(2,1)}, bf16[1024,384]{1,0:T(8,128)(2,1)}, bf16[512,768]{1,0:T(8,128)(2,1)}) custom-call(s32[1]{0:T(128)} %bitcast.1.refs_0_, f32[12,512]{1,0:T(8,128)} %bitcast.19, f32[512,128]{1,0:T(8,128)} %get-tuple-element.83.refs_2_.refs_0_, ...), custom_call_target="tpu_custom_call" | custom-call | flops 2359296 | bytes 196608 | tf_op jit(solution)/shard_map/attend/pallas_call | solution.py:199
  52.6 0.7 collective-permute-start.6
  53.3 2.7 %collective-permute-start.7 = (bf16[1024,384]{1,0:T(8,128)(2,1)}, bf16[1024,384]{1,0:T(8,128)(2,1)S(1)}, u32[]{:S(2)}, u32[]{:S(2)}) collective-permute-start(bf16[1024,384]{1,0:T(8,128)(2,1)} %get-tuple-element.96), channel_id=1, source_target_pairs={{4,8},{8,4},{12,16},{16,12},{20,24},{24,20},{28,32},{32,28},{36,40... | collective-permute-start | bytes 2359304 | tf_op jit(solution)/shard_map/ppermute | solution.py:30
  56.0 0.0 collective-permute-done.3.refs_10_.refs_11_
  56.0 0.0 copy-start.7
  56.0 0.0 collective-permute-done.2.refs_8_.refs_9_
  56.0 0.9 copy-done.7
  56.9 12.7 %attend.3 = (bf16[512,768]{1,0:T(8,128)(2,1)}, bf16[1024,384]{1,0:T(8,128)(2,1)}, bf16[1024,384]{1,0:T(8,128)(2,1)}, bf16[1024,384]{1,0:T(8,128)(2,1)}, bf16[512,768]{1,0:T(8,128)(2,1)}) custom-call(s32[1]{0:T(128)} %bitcast.1.refs_0_, f32[12,512]{1,0:T(8,128)} %bitcast.20, ...), custom_call_target="tpu_custom_call", output_to_operand_aliasing={{0}: (14, {}), {4}: (15, {})} | custom-call | flops 2359296 | bytes 196608 | tf_op jit(solution)/shard_map/attend/pallas_call | solution.py:199
  69.6 1.9 %collective-permute-start.4 = (bf16[1024,384]{1,0:T(8,128)(2,1)}, bf16[1024,384]{1,0:T(8,128)(2,1)}, u32[]{:S(2)}, u32[]{:S(2)}) collective-permute-start(bf16[1024,384]{1,0:T(8,128)(2,1)} %get-tuple-element.92), channel_id=1, source_target_pairs={{0,4},{4,0},{8,12},{12,8},{16,20},{20,16},{24,28},{28,24},{32,36},... | collective-permute-start | bytes 2359304 | tf_op jit(solution)/shard_map/ppermute | solution.py:30
  71.4 4.5 %collective-permute-start.5 = (bf16[1024,384]{1,0:T(8,128)(2,1)}, bf16[1024,384]{1,0:T(8,128)(2,1)}, u32[]{:S(2)}, u32[]{:S(2)}) collective-permute-start(bf16[1024,384]{1,0:T(8,128)(2,1)} %get-tuple-element.93), channel_id=1, source_target_pairs={{4,8},{8,4},{12,16},{16,12},{20,24},{24,20},{28,32},{32,28},{36,40... | collective-permute-start | bytes 2359304 | tf_op jit(solution)/shard_map/ppermute | solution.py:30
  75.9 1.2 %slice.37 = s32[1,1]{1,0:T(1,128)} slice(s32[128,128]{1,0:T(8,128)} %param.17), slice={[0:1], [0:1]} | slice | bytes 8 | tf_op jit(solution)/shard_map/slice | solution.py:305
  77.7 0.6 pad_maximum_fusion.4
  78.3 0.0 collective-permute-done.6.refs_4_.refs_5_
  78.4 0.0 collective-permute-done.7.refs_6_.refs_7_
  78.4 1.4 %finish.2 = (bf16[512,768]{1,0:T(8,128)(2,1)}, bf16[512,768]{1,0:T(8,128)(2,1)}) custom-call(f32[512,128]{1,0:T(8,128)S(1)} %copy-done.1, f32[512,128]{1,0:T(8,128)S(1)} %copy-done, bf16[1024,384]{1,0:T(8,128)(2,1)S(1)} %copy-done.2, bf16[1024,384]{1,0:T(8,128)(2,1)S(1)} %copy-done.2, bf16[1024,384]{1,0:T(8,128)(2,1)S(1)} %collective-permute-done.6.refs_4_.refs_5_, ...), custom_call_target="tpu_custom_call" | custom-call | flops 1966080 | bytes 3932160 | tf_op jit(solution)/shard_map/finish/pallas_call | solution.py:249
  79.8 30.5 %while.12 = (s32[]{:T(128)}, bf16[16,768]{1,0:T(8,128)(2,1)}, s32[]{:T(128)}, bf16[512,768]{1,0:T(8,128)(2,1)}, s32[]{:T(128)}, /*index=5*/bf16[]{:T(256)}) while((s32[]{:T(128)}, bf16[16,768]{1,0:T(8,128)(2,1)}, s32[]{:T(128)}, bf16[512,768]{1,0:T(8,128)(2,1)}, s32[]{:T(128)}, /*index=5*/bf16[]{:T(256)}) %tuple.41), condition=%wide.region_2.3_spmd, body=%wide.region_0.2_spmd.sunk | while | flops 380930 | bytes 3170407 | solution.py:306
  79.8 9.7 %all-to-all-start = ((bf16[32,16,768]{2,1,0:T(8,128)(2,1)}), bf16[32,16,768]{2,1,0:T(8,128)(2,1)S(1)}, u32[]{:S(2)}, u32[]{:S(2)}) async-start(bf16[32,16,768]{2,1,0:T(8,128)(2,1)} %bitcast.14), calls=%async_computation | async-start | bytes 1572864 | tf_op jit(solution)/shard_map/while/body/all_to_all | solution.py:302
  89.5 20.1 %all-to-all-done = bf16[32,16,768]{2,1,0:T(8,128)(2,1)S(1)} async-done(((bf16[32,16,768]{2,1,0:T(8,128)(2,1)}), bf16[32,16,768]{2,1,0:T(8,128)(2,1)S(1)}, u32[]{:S(2)}, u32[]{:S(2)}) %all-to-all-start) | async-done | bytes 786464 | tf_op jit(solution)/shard_map/while/body/all_to_all | solution.py:302
  109.5 0.7 reduce_sum.13
  110.3 1.3 %fusion.9 = (bf16[8,768]{1,0:T(8,128)(2,1)}, bf16[8,768]{1,0:T(8,128)(2,1)}) fusion(bf16[16,768]{1,0:T(8,128)(2,1)} %get-tuple-element.102), kind=kLoop, calls=%fused_computation.32 | loop fusion | bytes 49152 | tf_op jit(solution)/shard_map/slice | solution.py:308
  111.6 0.0 collective-permute-done.4.refs_4_.refs_5_
  111.6 0.0 collective-permute-done.5.refs_6_.refs_7_
  111.6 2.7 %finish.3 = (bf16[512,768]{1,0:T(8,128)(2,1)}, bf16[512,768]{1,0:T(8,128)(2,1)}) custom-call(f32[512,128]{1,0:T(8,128)S(1)} %copy-done.1, f32[512,128]{1,0:T(8,128)S(1)} %copy-done, bf16[1024,384]{1,0:T(8,128)(2,1)S(1)} %copy-done.3, bf16[1024,384]{1,0:T(8,128)(2,1)S(1)} %copy-done.3, ...), custom_call_target="tpu_custom_call", output_to_operand_aliasing={{0}: (8, {}), {1}: (9, {})} | custom-call | flops 1966080 | bytes 3932160 | tf_op jit(solution)/shard_map/finish/pallas_call | solution.py:249
  (32 shorter events, 0.1 us)
Async XLA Ops:
  0.6 1.0 slice-start
  0.6 1.1 slice-start.2
  1.8 7.6 %copy-start.12 = (s32[3,512]{1,0:T(4,128)S(1)}, s32[3,512]{1,0:T(4,128)}, u32[]{:S(2)}) copy-start(s32[3,512]{1,0:T(4,128)} %param.16) | copy-start | bytes 18436
  1.8 7.8 %copy-start.9 = (bf16[8,768]{1,0:T(8,128)(2,1)S(1)}, bf16[8,768]{1,0:T(8,128)(2,1)}, u32[]{:S(2)}) copy-start(bf16[8,768]{1,0:T(8,128)(2,1)} %param.15) | copy-start | bytes 36868
  1.8 7.8 %copy-start.10 = (bf16[8,768]{1,0:T(8,128)(2,1)S(1)}, bf16[8,768]{1,0:T(8,128)(2,1)}, u32[]{:S(2)}) copy-start(bf16[8,768]{1,0:T(8,128)(2,1)} %param.14) | copy-start | bytes 36868
  2.7 18.6 %collective-permute-start.1 = (bf16[1024,384]{1,0:T(8,128)(2,1)}, bf16[1024,384]{1,0:T(8,128)(2,1)S(1)}, u32[]{:S(2)}, u32[]{:S(2)}) collective-permute-start(bf16[1024,384]{1,0:T(8,128)(2,1)} %pad_maximum_fusion), channel_id=1, source_target_pairs={{0,4},{4,0},{8,12},{12,8},{16,20},{20,16},{24,28},{28,24},{32,36},... | collective-permute-start | bytes 2359304 | tf_op jit(solution)/shard_map/ppermute | solution.py:30
  3.3 26.9 %collective-permute-start = (bf16[1024,384]{1,0:T(8,128)(2,1)}, bf16[1024,384]{1,0:T(8,128)(2,1)S(1)}, u32[]{:S(2)}, u32[]{:S(2)}) collective-permute-start(bf16[1024,384]{1,0:T(8,128)(2,1)} %pad_maximum_fusion), channel_id=1, source_target_pairs={{4,8},{8,4},{12,16},{16,12},{20,24},{24,20},{28,32},{32,28},{36,40... | collective-permute-start | bytes 2359304 | tf_op jit(solution)/shard_map/ppermute | solution.py:30
  12.6 6.8 %copy-start.8 = (s32[128,128]{1,0:T(8,128)S(1)}, s32[128,128]{1,0:T(8,128)}, u32[]{:S(2)}) copy-start(s32[128,128]{1,0:T(8,128)} %param.17) | copy-start | bytes 196612
  12.6 26.5 %all-to-all-start.1 = ((bf16[32,8,1536]{2,1,0:T(8,128)(2,1)}), bf16[32,8,1536]{2,1,0:T(8,128)(2,1)S(1)}, u32[]{:S(2)}, u32[]{:S(2)}) async-start(bf16[32,8,1536]{2,1,0:T(8,128)(2,1)} %tile.2), calls=%async_computation.1 | async-start | bytes 1572864 | tf_op jit(solution)/shard_map/all_to_all | solution.py:279
  20.3 1.9 %slice-start.1 = ((bf16[512,768]{1,0:T(8,128)(2,1)}), bf16[512,384]{1,0:T(8,128)(2,1)S(1)}, s32[]{:S(2)}) async-start(bf16[512,768]{1,0:T(8,128)(2,1)} %refs_6_.3), calls=%async_computation.3 | async-start | bytes 786432 | tf_op jit(solution)/shard_map/slice | solution.py:275
  20.3 1.9 %slice-start.3 = ((bf16[512,768]{1,0:T(8,128)(2,1)}), bf16[512,384]{1,0:T(8,128)(2,1)S(1)}, s32[]{:S(2)}) async-start(bf16[512,768]{1,0:T(8,128)(2,1)} %refs_7_.3), calls=%async_computation.5 | async-start | bytes 786432 | tf_op jit(solution)/shard_map/slice | solution.py:275
  21.3 0.9 copy-start.5
  30.1 9.0 %copy-start.6 = (bf16[1024,384]{1,0:T(8,128)(2,1)}, bf16[1024,384]{1,0:T(8,128)(2,1)S(1)}, u32[]{:S(2)}) copy-start(bf16[1024,384]{1,0:T(8,128)(2,1)S(1)} %collective-permute-done.refs_10_.refs_11_) | copy-start | bytes 2359300
  30.1 25.8 %collective-permute-start.3 = (bf16[1024,384]{1,0:T(8,128)(2,1)}, bf16[1024,384]{1,0:T(8,128)(2,1)S(1)}, u32[]{:S(2)}, u32[]{:S(2)}) collective-permute-start(bf16[1024,384]{1,0:T(8,128)(2,1)} %pad_maximum_fusion.1), channel_id=1, source_target_pairs={{4,8},{8,4},{12,16},{16,12},{20,24},{24,20},{28,32},{32,28},{36,40... | collective-permute-start | bytes 2359304 | tf_op jit(solution)/shard_map/ppermute | solution.py:30
  38.2 17.8 %collective-permute-start.2 = (bf16[1024,384]{1,0:T(8,128)(2,1)}, bf16[1024,384]{1,0:T(8,128)(2,1)}, u32[]{:S(2)}, u32[]{:S(2)}) collective-permute-start(bf16[1024,384]{1,0:T(8,128)(2,1)} %pad_maximum_fusion.1), channel_id=1, source_target_pairs={{0,4},{4,0},{8,12},{12,8},{16,20},{20,16},{24,28},{28,24},{32,36},... | collective-permute-start | bytes 2359304 | tf_op jit(solution)/shard_map/ppermute | solution.py:30
  39.2 0.9 copy-start.4
  52.6 25.7 %collective-permute-start.6 = (bf16[1024,384]{1,0:T(8,128)(2,1)}, bf16[1024,384]{1,0:T(8,128)(2,1)S(1)}, u32[]{:S(2)}, u32[]{:S(2)}) collective-permute-start(bf16[1024,384]{1,0:T(8,128)(2,1)} %get-tuple-element.95), channel_id=1, source_target_pairs={{0,4},{4,0},{8,12},{12,8},{16,20},{20,16},{24,28},{28,24},{32,36},... | collective-permute-start | bytes 2359304 | tf_op jit(solution)/shard_map/ppermute | solution.py:30
  53.3 25.1 %collective-permute-start.7 = (bf16[1024,384]{1,0:T(8,128)(2,1)}, bf16[1024,384]{1,0:T(8,128)(2,1)S(1)}, u32[]{:S(2)}, u32[]{:S(2)}) collective-permute-start(bf16[1024,384]{1,0:T(8,128)(2,1)} %get-tuple-element.96), channel_id=1, source_target_pairs={{4,8},{8,4},{12,16},{16,12},{20,24},{24,20},{28,32},{32,28},{36,40... | collective-permute-start | bytes 2359304 | tf_op jit(solution)/shard_map/ppermute | solution.py:30
  56.0 0.9 copy-start.7
  56.9 20.9 %copy-start.11 = (bf16[8,768]{1,0:T(8,128)(2,1)S(1)}, bf16[8,768]{1,0:T(8,128)(2,1)}, u32[]{:S(2)}) copy-start(bf16[8,768]{1,0:T(8,128)(2,1)} %param.14) | copy-start | bytes 36868
  56.9 21.5 %copy-start = (f32[512,128]{1,0:T(8,128)S(1)}, f32[512,128]{1,0:T(8,128)}, u32[]{:S(2)}) copy-start(f32[512,128]{1,0:T(8,128)} %get-tuple-element.84.refs_3_.refs_1_) | copy-start | bytes 786436
  56.9 21.5 %copy-start.1 = (f32[512,128]{1,0:T(8,128)S(1)}, f32[512,128]{1,0:T(8,128)}, u32[]{:S(2)}) copy-start(f32[512,128]{1,0:T(8,128)} %get-tuple-element.83.refs_2_.refs_0_) | copy-start | bytes 786436
  56.9 21.5 %copy-start.2 = (bf16[1024,384]{1,0:T(8,128)(2,1)S(1)}, bf16[1024,384]{1,0:T(8,128)(2,1)}, u32[]{:S(2)}) copy-start(bf16[1024,384]{1,0:T(8,128)(2,1)} %get-tuple-element.94.refs_2_.refs_3_) | copy-start | bytes 2359300
  69.6 42.0 %collective-permute-start.4 = (bf16[1024,384]{1,0:T(8,128)(2,1)}, bf16[1024,384]{1,0:T(8,128)(2,1)}, u32[]{:S(2)}, u32[]{:S(2)}) collective-permute-start(bf16[1024,384]{1,0:T(8,128)(2,1)} %get-tuple-element.92), channel_id=1, source_target_pairs={{0,4},{4,0},{8,12},{12,8},{16,20},{20,16},{24,28},{28,24},{32,36},... | collective-permute-start | bytes 2359304 | tf_op jit(solution)/shard_map/ppermute | solution.py:30
  71.4 40.2 %collective-permute-start.5 = (bf16[1024,384]{1,0:T(8,128)(2,1)}, bf16[1024,384]{1,0:T(8,128)(2,1)}, u32[]{:S(2)}, u32[]{:S(2)}) collective-permute-start(bf16[1024,384]{1,0:T(8,128)(2,1)} %get-tuple-element.93), channel_id=1, source_target_pairs={{4,8},{8,4},{12,16},{16,12},{20,24},{24,20},{28,32},{32,28},{36,40... | collective-permute-start | bytes 2359304 | tf_op jit(solution)/shard_map/ppermute | solution.py:30
  79.8 31.8 %copy-start.3 = (bf16[1024,384]{1,0:T(8,128)(2,1)S(1)}, bf16[1024,384]{1,0:T(8,128)(2,1)}, u32[]{:S(2)}) copy-start(bf16[1024,384]{1,0:T(8,128)(2,1)} %get-tuple-element.91.refs_2_.refs_3_) | copy-start | bytes 2359300
  79.8 29.8 %all-to-all-start = ((bf16[32,16,768]{2,1,0:T(8,128)(2,1)}), bf16[32,16,768]{2,1,0:T(8,128)(2,1)S(1)}, u32[]{:S(2)}, u32[]{:S(2)}) async-start(bf16[32,16,768]{2,1,0:T(8,128)(2,1)} %bitcast.14), calls=%async_computation | async-start | bytes 1572864 | tf_op jit(solution)/shard_map/while/body/all_to_all | solution.py:302

commit v5 on v4

--- a/solution.py
+++ b/solution.py
@@ -120,7 +120,7 @@
             if frame not in frames:
                 continue
             dprobs = dot(v_ref[row:row + f, :], grad, NT)
-            dp_scr[c * f:(c + 1) * f, cols] = dprobs
+            dp_scr[c * f:(c + 1) * f, cols] = dprobs.astype(jnp.bfloat16)
             for t in range(2):
                 rows = slice(c * f + t * TILE, c * f + (t + 1) * TILE)
                 shift = top
@@ -146,7 +146,7 @@
         rows = slice(c * f, (c + 1) * f)
         cols = slice(frames[0] * f, (frames[-1] + 1) * f)
         weights = e_scr[rows, cols]
-        dscores = (weights.astype(jnp.float32) * (dp_scr[rows, cols] - delta_both[:, cols])).astype(jnp.bfloat16)
+        dscores = (weights.astype(jnp.float32) * (dp_scr[rows, cols].astype(jnp.float32) - delta_both[:, cols])).astype(jnp.bfloat16)
         value_term = dot(weights, g_both[cols], NN)
         key_term = dot(dscores, q_both[cols], NN)
         key = k_ref[row:row + f, :]
@@ -210,7 +210,7 @@
         ],
         scratch_shapes=[
             pltpu.VMEM((keys, tok), jnp.float32),
-            pltpu.VMEM((keys, tok), jnp.float32),
+            pltpu.VMEM((keys, tok), jnp.bfloat16),
             pltpu.VMEM((keys, tok), jnp.bfloat16),
         ] + [pltpu.VMEM((tok, D_HEAD), jnp.bfloat16)] * 4,
         input_output_aliases=aliases,

time: 116 us -> 115 us (level)
  no operation moved by 1% of the time
where the time goes in v5:
time: 115 us; the launch traced here: 114 us
  starting transfers between devices  40.8 us (35%)
  waiting for transfers between devices  29 us (25%)
  Pallas kernels  28.9 us (25%)
  local copies, waits for them, and re-layouts  8.02 us (7%)
  other arithmetic  5.59 us (5%)
  between operations  1.55 us (1%)
    pallas_call x2, Pallas kernels, attend(): pl.pallas_call(functools.partial(attend_body, aliased=before is not None,...  24.8 us
    ppermute x8, starting transfers between devices, exchange(): return lax.ppermute(block, axis, route)  24.4 us
    all_to_all x1, waiting for transfers between devices, reduce_text(): return part_sum(lax.all_to_all(rows, 'ctx', 0, 0, tiled=True), ctx_size)  20.1 us
    all_to_all x1, starting transfers between devices, reduce_text(): return part_sum(lax.all_to_all(rows, 'ctx', 0, 0, tiled=True), ctx_size)  9.65 us
    ppermute x8, waiting for transfers between devices, exchange(): return lax.ppermute(block, axis, route)  8.01 us
    all_to_all x1, starting transfers between devices, shards(): lax.all_to_all(jnp.tile(text_own, (ctx_size, 1)), 'ctx', 0, 0, tiled=True)  6.76 us
    pallas_call x2, Pallas kernels, finish(): pl.pallas_call(functools.partial(finish_body, aliased=before is not None)...  4.07 us
    unnamed x28, local copies, waits for them, and re-layouts  3.28 us
  transfers between devices with their start and end apart: 10, of which 4 were waited for; matrix products, arithmetic and copies ran while one was open for 8% of the time, Pallas kernels for 23%

profile of v5, /device:TPU:15, one launch (start us, length us, event | category | flops | bytes accessed | tf_op | source)
XLA Modules:
  0.0 113.8 jit_solution(13644321935730359280)
XLA Ops:
  0.6 0.0 slice-start
  0.6 0.0 slice-start.2
  0.7 1.0 slice-done
  1.6 0.1 slice-done.2
  1.8 1.0 pad_maximum_fusion
  2.7 0.5 collective-permute-start.1
  3.3 6.1 %collective-permute-start = (bf16[1024,384]{1,0:T(8,128)(2,1)}, bf16[1024,384]{1,0:T(8,128)(2,1)S(1)}, u32[]{:S(2)}, u32[]{:S(2)}) collective-permute-start(bf16[1024,384]{1,0:T(8,128)(2,1)} %pad_maximum_fusion), channel_id=1, source_target_pairs={{4,8},{8,4},{12,16},{16,12},{20,24},{24,20},{28,32},{32,28},{36,40... | collective-permute-start | bytes 2359304 | tf_op jit(solution)/shard_map/ppermute | solution.py:30
  9.3 0.0 copy-done.12
  9.4 0.1 broadcast_multiply_fusion.2
  9.6 0.2 broadcast_multiply_fusion.1
  9.8 1.9 %negate_select_fusion = (f32[512,128]{1,0:T(8,128)}, f32[512,128]{1,0:T(8,128)}) fusion(pred[128]{0:T(512)(128)(4,1)S(1)} %fusion.7, f32[512,56]{1,0:T(8,128)S(1)} %get-tuple-element.118, f32[512,56]{1,0:T(8,128)S(1)} %get-tuple-element.117, f32[512,16]{1,0:T(8,128)S(1)} %broadcast_multiply_fusion.2), kind=kLoop, calls=%fused_computation.2 | loop fusion | flops 262144 | bytes 786560 | tf_op jit(solution)/shard_map/jit(_where)/select_n | solution.py:63
  11.7 0.9 tile.2
  12.6 6.8 %all-to-all-start.1 = ((bf16[32,8,1536]{2,1,0:T(8,128)(2,1)}), bf16[32,8,1536]{2,1,0:T(8,128)(2,1)S(1)}, u32[]{:S(2)}, u32[]{:S(2)}) async-start(bf16[32,8,1536]{2,1,0:T(8,128)(2,1)} %tile.2), calls=%async_computation.1 | async-start | bytes 1572864 | tf_op jit(solution)/shard_map/all_to_all | solution.py:279
  19.4 0.1 select_bitcast_fusion
  19.5 0.1 copy.17
  19.6 0.1 broadcast_in_dim.33
  19.7 0.6 copy.18
  20.3 1.0 collective-permute-done.1.refs_8_.refs_9_
  21.3 0.9 copy-done.5
  22.2 1.0 pad_maximum_fusion.1
  23.2 7.0 %collective-permute-done.refs_10_.refs_11_ = bf16[1024,384]{1,0:T(8,128)(2,1)S(1)} collective-permute-done((bf16[1024,384]{1,0:T(8,128)(2,1)}, bf16[1024,384]{1,0:T(8,128)(2,1)S(1)}, u32[]{:S(2)}, u32[]{:S(2)}) %collective-permute-start) | collective-permute-done | bytes 786464 | tf_op jit(solution)/shard_map/ppermute | solution.py:30
  30.1 8.1 %collective-permute-start.3 = (bf16[1024,384]{1,0:T(8,128)(2,1)}, bf16[1024,384]{1,0:T(8,128)(2,1)S(1)}, u32[]{:S(2)}, u32[]{:S(2)}) collective-permute-start(bf16[1024,384]{1,0:T(8,128)(2,1)} %pad_maximum_fusion.1), channel_id=1, source_target_pairs={{4,8},{8,4},{12,16},{16,12},{20,24},{24,20},{28,32},{32,28},{36,40... | collective-permute-start | bytes 2359304 | tf_op jit(solution)/shard_map/ppermute | solution.py:30
  38.2 0.1 collective-permute-start.2
  38.3 0.9 all-to-all-done.1
  39.2 0.9 copy-done.4
  40.1 12.3 %attend.2 = (bf16[512,768]{1,0:T(8,128)(2,1)}, bf16[1024,384]{1,0:T(8,128)(2,1)}, bf16[1024,384]{1,0:T(8,128)(2,1)}, bf16[1024,384]{1,0:T(8,128)(2,1)}, bf16[512,768]{1,0:T(8,128)(2,1)}) custom-call(s32[1]{0:T(128)} %bitcast.1.refs_0_, f32[12,512]{1,0:T(8,128)} %bitcast.19, f32[512,128]{1,0:T(8,128)} %get-tuple-element.83.refs_2_.refs_0_, ...), custom_call_target="tpu_custom_call" | custom-call | flops 2359296 | bytes 196608 | tf_op jit(solution)/shard_map/attend/pallas_call | solution.py:199
  52.4 0.7 collective-permute-start.6
  53.1 2.7 %collective-permute-start.7 = (bf16[1024,384]{1,0:T(8,128)(2,1)}, bf16[1024,384]{1,0:T(8,128)(2,1)S(1)}, u32[]{:S(2)}, u32[]{:S(2)}) collective-permute-start(bf16[1024,384]{1,0:T(8,128)(2,1)} %get-tuple-element.96), channel_id=1, source_target_pairs={{4,8},{8,4},{12,16},{16,12},{20,24},{24,20},{28,32},{32,28},{36,40... | collective-permute-start | bytes 2359304 | tf_op jit(solution)/shard_map/ppermute | solution.py:30
  55.7 0.0 collective-permute-done.3.refs_10_.refs_11_
  55.8 0.0 copy-start.7
  55.8 0.0 collective-permute-done.2.refs_8_.refs_9_
  55.8 0.9 copy-done.7
  56.7 12.5 %attend.3 = (bf16[512,768]{1,0:T(8,128)(2,1)}, bf16[1024,384]{1,0:T(8,128)(2,1)}, bf16[1024,384]{1,0:T(8,128)(2,1)}, bf16[1024,384]{1,0:T(8,128)(2,1)}, bf16[512,768]{1,0:T(8,128)(2,1)}) custom-call(s32[1]{0:T(128)} %bitcast.1.refs_0_, f32[12,512]{1,0:T(8,128)} %bitcast.20, ...), custom_call_target="tpu_custom_call", output_to_operand_aliasing={{0}: (14, {}), {4}: (15, {})} | custom-call | flops 2359296 | bytes 196608 | tf_op jit(solution)/shard_map/attend/pallas_call | solution.py:199
  69.1 1.8 %collective-permute-start.4 = (bf16[1024,384]{1,0:T(8,128)(2,1)}, bf16[1024,384]{1,0:T(8,128)(2,1)}, u32[]{:S(2)}, u32[]{:S(2)}) collective-permute-start(bf16[1024,384]{1,0:T(8,128)(2,1)} %get-tuple-element.92), channel_id=1, source_target_pairs={{0,4},{4,0},{8,12},{12,8},{16,20},{20,16},{24,28},{28,24},{32,36},... | collective-permute-start | bytes 2359304 | tf_op jit(solution)/shard_map/ppermute | solution.py:30
  71.0 4.5 %collective-permute-start.5 = (bf16[1024,384]{1,0:T(8,128)(2,1)}, bf16[1024,384]{1,0:T(8,128)(2,1)}, u32[]{:S(2)}, u32[]{:S(2)}) collective-permute-start(bf16[1024,384]{1,0:T(8,128)(2,1)} %get-tuple-element.93), channel_id=1, source_target_pairs={{4,8},{8,4},{12,16},{16,12},{20,24},{24,20},{28,32},{32,28},{36,40... | collective-permute-start | bytes 2359304 | tf_op jit(solution)/shard_map/ppermute | solution.py:30
  75.4 1.2 %slice.37 = s32[1,1]{1,0:T(1,128)} slice(s32[128,128]{1,0:T(8,128)} %param.17), slice={[0:1], [0:1]} | slice | bytes 8 | tf_op jit(solution)/shard_map/slice | solution.py:305
  77.3 0.6 pad_maximum_fusion.4
  77.9 0.0 collective-permute-done.6.refs_4_.refs_5_
  77.9 0.0 collective-permute-done.7.refs_6_.refs_7_
  77.9 1.4 %finish.2 = (bf16[512,768]{1,0:T(8,128)(2,1)}, bf16[512,768]{1,0:T(8,128)(2,1)}) custom-call(f32[512,128]{1,0:T(8,128)S(1)} %copy-done.1, f32[512,128]{1,0:T(8,128)S(1)} %copy-done, bf16[1024,384]{1,0:T(8,128)(2,1)S(1)} %copy-done.2, bf16[1024,384]{1,0:T(8,128)(2,1)S(1)} %copy-done.2, bf16[1024,384]{1,0:T(8,128)(2,1)S(1)} %collective-permute-done.6.refs_4_.refs_5_, ...), custom_call_target="tpu_custom_call" | custom-call | flops 1966080 | bytes 3932160 | tf_op jit(solution)/shard_map/finish/pallas_call | solution.py:249
  79.4 30.5 %while.12 = (s32[]{:T(128)}, bf16[16,768]{1,0:T(8,128)(2,1)}, s32[]{:T(128)}, bf16[512,768]{1,0:T(8,128)(2,1)}, s32[]{:T(128)}, /*index=5*/bf16[]{:T(256)}) while((s32[]{:T(128)}, bf16[16,768]{1,0:T(8,128)(2,1)}, s32[]{:T(128)}, bf16[512,768]{1,0:T(8,128)(2,1)}, s32[]{:T(128)}, /*index=5*/bf16[]{:T(256)}) %tuple.41), condition=%wide.region_2.3_spmd, body=%wide.region_0.2_spmd.sunk | while | flops 380930 | bytes 3170407 | solution.py:306
  79.4 9.7 %all-to-all-start = ((bf16[32,16,768]{2,1,0:T(8,128)(2,1)}), bf16[32,16,768]{2,1,0:T(8,128)(2,1)S(1)}, u32[]{:S(2)}, u32[]{:S(2)}) async-start(bf16[32,16,768]{2,1,0:T(8,128)(2,1)} %bitcast.14), calls=%async_computation | async-start | bytes 1572864 | tf_op jit(solution)/shard_map/while/body/all_to_all | solution.py:302
  89.0 20.1 %all-to-all-done = bf16[32,16,768]{2,1,0:T(8,128)(2,1)S(1)} async-done(((bf16[32,16,768]{2,1,0:T(8,128)(2,1)}), bf16[32,16,768]{2,1,0:T(8,128)(2,1)S(1)}, u32[]{:S(2)}, u32[]{:S(2)}) %all-to-all-start) | async-done | bytes 786464 | tf_op jit(solution)/shard_map/while/body/all_to_all | solution.py:302
  109.1 0.7 reduce_sum.13
  109.8 1.3 %fusion.9 = (bf16[8,768]{1,0:T(8,128)(2,1)}, bf16[8,768]{1,0:T(8,128)(2,1)}) fusion(bf16[16,768]{1,0:T(8,128)(2,1)} %get-tuple-element.102), kind=kLoop, calls=%fused_computation.32 | loop fusion | bytes 49152 | tf_op jit(solution)/shard_map/slice | solution.py:308
  111.2 0.0 collective-permute-done.4.refs_4_.refs_5_
  111.2 0.0 collective-permute-done.5.refs_6_.refs_7_
  111.2 2.7 %finish.3 = (bf16[512,768]{1,0:T(8,128)(2,1)}, bf16[512,768]{1,0:T(8,128)(2,1)}) custom-call(f32[512,128]{1,0:T(8,128)S(1)} %copy-done.1, f32[512,128]{1,0:T(8,128)S(1)} %copy-done, bf16[1024,384]{1,0:T(8,128)(2,1)S(1)} %copy-done.3, bf16[1024,384]{1,0:T(8,128)(2,1)S(1)} %copy-done.3, ...), custom_call_target="tpu_custom_call", output_to_operand_aliasing={{0}: (8, {}), {1}: (9, {})} | custom-call | flops 1966080 | bytes 3932160 | tf_op jit(solution)/shard_map/finish/pallas_call | solution.py:249
  (32 shorter events, 0.1 us)
Async XLA Ops:
  0.6 1.0 slice-start
  0.6 1.1 slice-start.2
  1.8 7.6 %copy-start.12 = (s32[3,512]{1,0:T(4,128)S(1)}, s32[3,512]{1,0:T(4,128)}, u32[]{:S(2)}) copy-start(s32[3,512]{1,0:T(4,128)} %param.16) | copy-start | bytes 18436
  1.8 7.8 %copy-start.9 = (bf16[8,768]{1,0:T(8,128)(2,1)S(1)}, bf16[8,768]{1,0:T(8,128)(2,1)}, u32[]{:S(2)}) copy-start(bf16[8,768]{1,0:T(8,128)(2,1)} %param.15) | copy-start | bytes 36868
  1.8 7.8 %copy-start.10 = (bf16[8,768]{1,0:T(8,128)(2,1)S(1)}, bf16[8,768]{1,0:T(8,128)(2,1)}, u32[]{:S(2)}) copy-start(bf16[8,768]{1,0:T(8,128)(2,1)} %param.14) | copy-start | bytes 36868
  2.7 18.6 %collective-permute-start.1 = (bf16[1024,384]{1,0:T(8,128)(2,1)}, bf16[1024,384]{1,0:T(8,128)(2,1)S(1)}, u32[]{:S(2)}, u32[]{:S(2)}) collective-permute-start(bf16[1024,384]{1,0:T(8,128)(2,1)} %pad_maximum_fusion), channel_id=1, source_target_pairs={{0,4},{4,0},{8,12},{12,8},{16,20},{20,16},{24,28},{28,24},{32,36},... | collective-permute-start | bytes 2359304 | tf_op jit(solution)/shard_map/ppermute | solution.py:30
  3.3 26.9 %collective-permute-start = (bf16[1024,384]{1,0:T(8,128)(2,1)}, bf16[1024,384]{1,0:T(8,128)(2,1)S(1)}, u32[]{:S(2)}, u32[]{:S(2)}) collective-permute-start(bf16[1024,384]{1,0:T(8,128)(2,1)} %pad_maximum_fusion), channel_id=1, source_target_pairs={{4,8},{8,4},{12,16},{16,12},{20,24},{24,20},{28,32},{32,28},{36,40... | collective-permute-start | bytes 2359304 | tf_op jit(solution)/shard_map/ppermute | solution.py:30
  12.6 6.8 %copy-start.8 = (s32[128,128]{1,0:T(8,128)S(1)}, s32[128,128]{1,0:T(8,128)}, u32[]{:S(2)}) copy-start(s32[128,128]{1,0:T(8,128)} %param.17) | copy-start | bytes 196612
  12.6 26.5 %all-to-all-start.1 = ((bf16[32,8,1536]{2,1,0:T(8,128)(2,1)}), bf16[32,8,1536]{2,1,0:T(8,128)(2,1)S(1)}, u32[]{:S(2)}, u32[]{:S(2)}) async-start(bf16[32,8,1536]{2,1,0:T(8,128)(2,1)} %tile.2), calls=%async_computation.1 | async-start | bytes 1572864 | tf_op jit(solution)/shard_map/all_to_all | solution.py:279
  20.3 1.9 %slice-start.1 = ((bf16[512,768]{1,0:T(8,128)(2,1)}), bf16[512,384]{1,0:T(8,128)(2,1)S(1)}, s32[]{:S(2)}) async-start(bf16[512,768]{1,0:T(8,128)(2,1)} %refs_6_.3), calls=%async_computation.3 | async-start | bytes 786432 | tf_op jit(solution)/shard_map/slice | solution.py:275
  20.3 1.9 %slice-start.3 = ((bf16[512,768]{1,0:T(8,128)(2,1)}), bf16[512,384]{1,0:T(8,128)(2,1)S(1)}, s32[]{:S(2)}) async-start(bf16[512,768]{1,0:T(8,128)(2,1)} %refs_7_.3), calls=%async_computation.5 | async-start | bytes 786432 | tf_op jit(solution)/shard_map/slice | solution.py:275
  21.3 0.9 copy-start.5
  30.1 9.0 %copy-start.6 = (bf16[1024,384]{1,0:T(8,128)(2,1)}, bf16[1024,384]{1,0:T(8,128)(2,1)S(1)}, u32[]{:S(2)}) copy-start(bf16[1024,384]{1,0:T(8,128)(2,1)S(1)} %collective-permute-done.refs_10_.refs_11_) | copy-start | bytes 2359300
  30.1 25.6 %collective-permute-start.3 = (bf16[1024,384]{1,0:T(8,128)(2,1)}, bf16[1024,384]{1,0:T(8,128)(2,1)S(1)}, u32[]{:S(2)}, u32[]{:S(2)}) collective-permute-start(bf16[1024,384]{1,0:T(8,128)(2,1)} %pad_maximum_fusion.1), channel_id=1, source_target_pairs={{4,8},{8,4},{12,16},{16,12},{20,24},{24,20},{28,32},{32,28},{36,40... | collective-permute-start | bytes 2359304 | tf_op jit(solution)/shard_map/ppermute | solution.py:30
  38.2 17.6 %collective-permute-start.2 = (bf16[1024,384]{1,0:T(8,128)(2,1)}, bf16[1024,384]{1,0:T(8,128)(2,1)}, u32[]{:S(2)}, u32[]{:S(2)}) collective-permute-start(bf16[1024,384]{1,0:T(8,128)(2,1)} %pad_maximum_fusion.1), channel_id=1, source_target_pairs={{0,4},{4,0},{8,12},{12,8},{16,20},{20,16},{24,28},{28,24},{32,36},... | collective-permute-start | bytes 2359304 | tf_op jit(solution)/shard_map/ppermute | solution.py:30
  39.2 0.9 copy-start.4
  52.4 25.5 %collective-permute-start.6 = (bf16[1024,384]{1,0:T(8,128)(2,1)}, bf16[1024,384]{1,0:T(8,128)(2,1)S(1)}, u32[]{:S(2)}, u32[]{:S(2)}) collective-permute-start(bf16[1024,384]{1,0:T(8,128)(2,1)} %get-tuple-element.95), channel_id=1, source_target_pairs={{0,4},{4,0},{8,12},{12,8},{16,20},{20,16},{24,28},{28,24},{32,36},... | collective-permute-start | bytes 2359304 | tf_op jit(solution)/shard_map/ppermute | solution.py:30
  53.1 24.9 %collective-permute-start.7 = (bf16[1024,384]{1,0:T(8,128)(2,1)}, bf16[1024,384]{1,0:T(8,128)(2,1)S(1)}, u32[]{:S(2)}, u32[]{:S(2)}) collective-permute-start(bf16[1024,384]{1,0:T(8,128)(2,1)} %get-tuple-element.96), channel_id=1, source_target_pairs={{4,8},{8,4},{12,16},{16,12},{20,24},{24,20},{28,32},{32,28},{36,40... | collective-permute-start | bytes 2359304 | tf_op jit(solution)/shard_map/ppermute | solution.py:30
  55.8 0.9 copy-start.7
  56.6 20.7 %copy-start.11 = (bf16[8,768]{1,0:T(8,128)(2,1)S(1)}, bf16[8,768]{1,0:T(8,128)(2,1)}, u32[]{:S(2)}) copy-start(bf16[8,768]{1,0:T(8,128)(2,1)} %param.14) | copy-start | bytes 36868
  56.6 21.3 %copy-start = (f32[512,128]{1,0:T(8,128)S(1)}, f32[512,128]{1,0:T(8,128)}, u32[]{:S(2)}) copy-start(f32[512,128]{1,0:T(8,128)} %get-tuple-element.84.refs_3_.refs_1_) | copy-start | bytes 786436
  56.6 21.3 %copy-start.1 = (f32[512,128]{1,0:T(8,128)S(1)}, f32[512,128]{1,0:T(8,128)}, u32[]{:S(2)}) copy-start(f32[512,128]{1,0:T(8,128)} %get-tuple-element.83.refs_2_.refs_0_) | copy-start | bytes 786436
  56.6 21.3 %copy-start.2 = (bf16[1024,384]{1,0:T(8,128)(2,1)S(1)}, bf16[1024,384]{1,0:T(8,128)(2,1)}, u32[]{:S(2)}) copy-start(bf16[1024,384]{1,0:T(8,128)(2,1)} %get-tuple-element.94.refs_2_.refs_3_) | copy-start | bytes 2359300
  69.1 42.0 %collective-permute-start.4 = (bf16[1024,384]{1,0:T(8,128)(2,1)}, bf16[1024,384]{1,0:T(8,128)(2,1)}, u32[]{:S(2)}, u32[]{:S(2)}) collective-permute-start(bf16[1024,384]{1,0:T(8,128)(2,1)} %get-tuple-element.92), channel_id=1, source_target_pairs={{0,4},{4,0},{8,12},{12,8},{16,20},{20,16},{24,28},{28,24},{32,36},... | collective-permute-start | bytes 2359304 | tf_op jit(solution)/shard_map/ppermute | solution.py:30
  71.0 40.2 %collective-permute-start.5 = (bf16[1024,384]{1,0:T(8,128)(2,1)}, bf16[1024,384]{1,0:T(8,128)(2,1)}, u32[]{:S(2)}, u32[]{:S(2)}) collective-permute-start(bf16[1024,384]{1,0:T(8,128)(2,1)} %get-tuple-element.93), channel_id=1, source_target_pairs={{4,8},{8,4},{12,16},{16,12},{20,24},{24,20},{28,32},{32,28},{36,40... | collective-permute-start | bytes 2359304 | tf_op jit(solution)/shard_map/ppermute | solution.py:30
  79.4 31.8 %copy-start.3 = (bf16[1024,384]{1,0:T(8,128)(2,1)S(1)}, bf16[1024,384]{1,0:T(8,128)(2,1)}, u32[]{:S(2)}) copy-start(bf16[1024,384]{1,0:T(8,128)(2,1)} %get-tuple-element.91.refs_2_.refs_3_) | copy-start | bytes 2359300
  79.4 29.7 %all-to-all-start = ((bf16[32,16,768]{2,1,0:T(8,128)(2,1)}), bf16[32,16,768]{2,1,0:T(8,128)(2,1)S(1)}, u32[]{:S(2)}, u32[]{:S(2)}) async-start(bf16[32,16,768]{2,1,0:T(8,128)(2,1)} %bitcast.14), calls=%async_computation | async-start | bytes 1572864 | tf_op jit(solution)/shard_map/while/body/all_to_all | solution.py:302
